TPU v7x, 32 devices: a whole 2x2x4 slice. The times are simulated.
32 devices in a mesh: row: 4 (over z), col: 8 (over y, x, core).
Axes of the slice: x: 2, y: 2, z: 4, core: 2. Of those that a mesh axis runs over, the one named last changes fastest.
Arguments:
- source_tiles: bfloat16 [4, 8, 1024, 128], P('row', 'col'), may hold values from -6 to 6
- requests: int32 [4, 8, 8, 256], P('row', 'col'), may hold values from 0 to 1023
- stencil: int32 [128, 256, 4], P('row', 'col'), may hold values from 0 to 2047, as said below
- regrid_weight: float32 [128, 256, 4], P('row', 'col'), may hold values from 0.1 to 0.6
- w_in: bfloat16 [3, 3, 64, 128], replicated, may hold values from -0.4375 to 0.4375
- w_enc: bfloat16 [3, 3, 128, 128], replicated, may hold values from -0.3125 to 0.3125
- w_mid_first: bfloat16 [3, 3, 128, 128], replicated, may hold values from -0.3125 to 0.3125
- w_mid_second: bfloat16 [3, 3, 128, 128], replicated, may hold values from -0.3125 to 0.3125
- w_dec_first: bfloat16 [3, 3, 256, 128], replicated, may hold values from -0.21875 to 0.21875
- w_dec_second: bfloat16 [3, 3, 128, 128], replicated, may hold values from -0.3125 to 0.3125
- w_out: bfloat16 [128, 64], replicated, may hold values from -0.75 to 0.75
Outputs:
- forecast: bfloat16 [128, 256, 2, 64], P('row', 'col')
Inputs may be any that keep to these rules, and one draw needn't show every extreme that they name: `stencil`: within each device's 32 x 32 block of target cells, every slot 0 to 2047 appears at least once among the entries.
All inputs are finite; a program needn't handle non-finite values.
Results may differ from a plain program's by a relative error of at most 0.017.
Values may be sent and summed in bfloat16 or wider, within the bound.
A program may use at most 64 MiB of HBM per device.

v0:
```python
import jax
import jax.numpy as jnp
from jax import lax
from jax.sharding import PartitionSpec as P

FIELDS = 64
CH = 128


def with_halo(x, sides, width):
    for axis, dim in sides:
        devices, length = (lax.axis_size(axis), x.shape[dim])
        up = [(i, (i + 1) % devices) for i in range(devices)]
        down = [(j, i) for i, j in up]
        last = lax.slice_in_dim(x, length - width, length, axis=dim)
        leading = lax.slice_in_dim(x, 0, width, axis=dim)
        before = lax.ppermute(last, axis, up)
        after = lax.ppermute(leading, axis, down)
        x = jnp.concatenate([before, x, after], axis=dim)
    return x


def conv_valid(padded, weight):
    height = padded.shape[0] - 2
    width = padded.shape[1] - 2
    samples = padded.shape[2]
    inner = padded.shape[3]
    outer = weight.shape[3]
    total = jnp.zeros((height * width * samples, outer), jnp.float32)
    for row_step in range(3):
        for col_step in range(3):
            window = padded[row_step : row_step + height, col_step : col_step + width].reshape(
                -1, inner
            )
            total = total + jnp.dot(
                window, weight[row_step, col_step], preferred_element_type=jnp.float32
            )
    return jax.nn.silu(total).reshape(height, width, samples, outer).astype(jnp.bfloat16)


def rim_clear(padded, depth, rows_dev):
    global_rows = (
        lax.axis_index("row") * rows_dev + jnp.arange(padded.shape[0], dtype=jnp.int32) - depth
    )
    inside = (global_rows >= 0) & (global_rows < lax.axis_size("row") * rows_dev)
    return jnp.where(inside[:, None, None, None], padded, jnp.zeros_like(padded))


def body(
    source_tiles,
    requests,
    stencil,
    regrid_weight,
    w_in,
    w_enc,
    w_mid_first,
    w_mid_second,
    w_dec_first,
    w_dec_second,
    w_out,
):
    tile_rows = stencil.shape[0]
    tile_cols = stencil.shape[1]
    columns = source_tiles.shape[3]
    samples = columns // FIELDS
    cells = source_tiles.shape[2]
    groups = requests.shape[2]
    capacity = requests.shape[3]
    wanted = requests.reshape(groups, capacity)
    global_ids = (jnp.arange(groups, dtype=jnp.int32)[:, None] * cells + wanted).reshape(-1)
    empty = jnp.zeros((groups * capacity, columns), jnp.bfloat16)
    flattened = lax.all_gather(source_tiles, "col", axis=1, tiled=True).reshape(-1, columns)
    inside = (global_ids >= 0) & (global_ids < flattened.shape[0])
    picked = flattened[jnp.clip(global_ids, 0, flattened.shape[0] - 1)]
    buffer = jnp.where(inside[:, None], picked, empty)
    picked = buffer[stencil]
    regridded = jnp.sum(picked.astype(jnp.float32) * regrid_weight[..., None], axis=2).astype(
        jnp.bfloat16
    )
    regridded = regridded.reshape(tile_rows, tile_cols, samples, FIELDS)
    padded = rim_clear(with_halo(regridded, (("row", 0), ("col", 1)), 1), 1, tile_rows)
    first = conv_valid(padded, w_in)
    padded = rim_clear(with_halo(first, (("row", 0), ("col", 1)), 1), 1, tile_rows)
    skip = conv_valid(padded, w_enc)
    half_rows = tile_rows // 2
    half_cols = tile_cols // 2
    pooled = (
        skip.astype(jnp.float32)
        .reshape(half_rows, 2, half_cols, 2, samples, CH)
        .mean(axis=(1, 3))
        .astype(jnp.bfloat16)
    )
    padded = rim_clear(with_halo(pooled, (("row", 0), ("col", 1)), 1), 1, half_rows)
    middle = conv_valid(padded, w_mid_first)
    padded = rim_clear(with_halo(middle, (("row", 0), ("col", 1)), 1), 1, half_rows)
    coarse = conv_valid(padded, w_mid_second)
    upsampled = jnp.repeat(jnp.repeat(coarse, 2, axis=0), 2, axis=1)
    joined = jnp.concatenate([upsampled, skip], axis=-1)
    padded = rim_clear(with_halo(joined, (("row", 0), ("col", 1)), 1), 1, tile_rows)
    decoded_first = conv_valid(padded, w_dec_first)
    padded = rim_clear(with_halo(decoded_first, (("row", 0), ("col", 1)), 1), 1, tile_rows)
    decoded = conv_valid(padded, w_dec_second)
    result = jnp.dot(decoded.reshape(-1, CH), w_out, preferred_element_type=jnp.float32)
    return result.reshape(tile_rows, tile_cols, samples, FIELDS).astype(jnp.bfloat16)


def solution(mesh):
    placed = (
        P("row", "col", None, None),
        P("row", "col", None, None),
        P("row", "col", None),
        P("row", "col", None),
        P(),
        P(),
        P(),
        P(),
        P(),
        P(),
        P(),
    )
    return jax.shard_map(
        body, mesh=mesh, in_specs=placed, out_specs=P("row", "col", None, None), check_vma=False
    )
```

profile of v0, /device:TPU:0, one launch (start us, length us, event | category | flops | bytes accessed | tf_op | source)
XLA Modules:
  0.0 215.6 jit_solution(13235562589627824381)
XLA Ops:
  11.3 28.5 %all-gather.2.cloned.1.call-done = bf16[1,8,1024,128]{3,2,0,1:T(8,128)(2,1)} async-done(((bf16[1,1,1024,128]{3,2,0,1:T(8,128)(2,1)}), bf16[1,8,1024,128]{3,2,0,1:T(8,128)(2,1)}) %all-gather.2.cloned.1.call-update) | async-done | bytes 2097168 | tf_op jit(solution)/shard_map/all_gather | solution.py:72
  39.9 7.5 %gather_fusion = bf16[2048,128]{1,0:T(8,128)(2,1)S(1)} fusion(bf16[8192,128]{1,0:T(8,128)(2,1)} %bitcast.301, s32[2048]{0:T(1024)S(1)} %broadcast_clamp_fusion.1), kind=kCustom, calls=%fused_computation | custom fusion | bytes 1056768 | tf_op jit(solution)/shard_map/gather | solution.py:74
  47.7 12.1 %gather_fusion.1 = bf16[4096,128]{1,0:T(8,128)(2,1)S(1)} fusion(bf16[2048,128]{1,0:T(8,128)(2,1)S(1)} %broadcast_select_fusion.4, s32[4096]{0:T(1024)S(1)} %broadcast_clamp_fusion), kind=kCustom, calls=%fused_computation.1 | custom fusion | bytes 2113536 | tf_op jit(solution)/shard_map/gather | solution.py:76
  59.8 1.6 fusion
  61.5 1.5 collective-permute-start
  63.4 2.3 %collective-permute-start.1 = (bf16[1,32,2,64]{3,2,1,0:T(2,128)(2,1)S(1)}, bf16[1,32,2,64]{3,2,1,0:T(2,128)(2,1)S(1)}, u32[]{:S(2)}, u32[]{:S(2)}) collective-permute-start(bf16[1,32,2,64]{3,2,1,0:T(2,128)(2,1)S(1)} %slice.423), channel_id=1, source_target_pairs={{8,0},{16,8},{24,16},{0,24},{9,1},{17,9},{25,17},{1,25},{10,2},{18... | collective-permute-start | bytes 24584 | tf_op jit(solution)/shard_map/ppermute | solution.py:18
  65.7 1.6 collective-permute-done
  67.9 2.6 %collective-permute-start.3 = (bf16[34,1,2,64]{3,2,1,0:T(2,128)(2,1)S(1)}, bf16[34,1,2,64]{3,2,1,0:T(2,128)(2,1)S(1)}, u32[]{:S(2)}, u32[]{:S(2)}) collective-permute-start(bf16[34,1,2,64]{3,2,1,0:T(2,128)(2,1)S(1)} %get-tuple-element.50), channel_id=1, source_target_pairs={{1,0},{2,1},{3,2},{4,3},{5,4},{6,5},{7,6},{0,7},{9,8},{10,9},{11,1... | collective-permute-start | bytes 26120 | tf_op jit(solution)/shard_map/ppermute | solution.py:18
  70.6 1.4 collective-permute-done.2
  73.1 5.2 %fusion.120 = (bf16[32,32,2,64]{3,2,1,0:T(2,128)(2,1)S(1)}, bf16[32,32,2,64]{3,2,1,0:T(2,128)(2,1)S(1)}, bf16[32,32,2,64]{3,2,1,0:T(2,128)(2,1)S(1)}, bf16[32,32...) fusion(bf16[34,34,2,64]{3,2,1,0:T(2,128)(2,1)S(1)} %broadcast_s, ...), kind=kLoop, calls=%fused_computation.218 | loop fusion | bytes 4718592 | tf_op jit(solution)/shard_map/slice | solution.py:32
  81.0 3.5 %collective-permute-start.5 = (bf16[1,32,2,128]{3,2,1,0:T(2,128)(2,1)S(1)}, bf16[1,32,2,128]{3,2,1,0:T(2,128)(2,1)S(1)}, u32[]{:S(2)}, u32[]{:S(2)}) collective-permute-start(bf16[1,32,2,128]{3,2,1,0:T(2,128)(2,1)S(1)} %bitcast.373), channel_id=1, source_target_pairs={{8,0},{16,8},{24,16},{0,24},{9,1},{17,9},{25,17},{1,25},{10,2},{18... | collective-permute-start | bytes 49160 | tf_op jit(solution)/shard_map/ppermute | solution.py:18
  84.5 1.4 collective-permute-done.5
  85.9 4.1 %collective-permute-done.4 = bf16[1,32,2,128]{3,2,1,0:T(2,128)(2,1)S(1)} collective-permute-done((bf16[1,32,2,128]{3,2,1,0:T(2,128)(2,1)S(1)}, bf16[1,32,2,128]{3,2,1,0:T(2,128)(2,1)S(1)}, u32[]{:S(2)}, u32[]{:S(2)}) %collective-permute-start.4) | collective-permute-done | bytes 16416 | tf_op jit(solution)/shard_map/ppermute | solution.py:17
  90.2 2.6 %collective-permute-start.7 = (bf16[34,1,2,128]{3,2,1,0:T(2,128)(2,1)S(1)}, bf16[34,1,2,128]{3,2,1,0:T(2,128)(2,1)S(1)}, u32[]{:S(2)}, u32[]{:S(2)}) collective-permute-start(bf16[34,1,2,128]{3,2,1,0:T(2,128)(2,1)S(1)} %get-tuple-element.48), channel_id=1, source_target_pairs={{1,0},{2,1},{3,2},{4,3},{5,4},{6,5},{7,6},{0,7},{9,8},{10,9},{11,1... | collective-permute-start | bytes 52232 | tf_op jit(solution)/shard_map/ppermute | solution.py:18
  92.8 1.6 collective-permute-done.6
  94.4 1.7 broadcast_select_fusion.3
  96.1 5.2 %fusion.119 = (bf16[32,32,2,128]{3,2,1,0:T(2,128)(2,1)S(1)}, bf16[32,32,2,128]{3,2,1,0:T(2,128)(2,1)S(1)}, bf16[32,32,2,128]{3,2,1,0:T(2,128)(2,1)S(1)}, bf16[32...) fusion(bf16[34,34,2,128]{3,2,1,0:T(2,128)(2,1)S(1)} %broadcast_, ...), kind=kLoop, calls=%fused_computation.217 | loop fusion | bytes 9437184 | tf_op jit(solution)/shard_map/slice | solution.py:32
  104.9 3.8 %collective-permute-start.9 = (bf16[1,16,2,128]{3,2,1,0:T(2,128)(2,1)S(1)}, bf16[1,16,2,128]{3,2,1,0:T(2,128)(2,1)S(1)}, u32[]{:S(2)}, u32[]{:S(2)}) collective-permute-start(bf16[1,16,2,128]{3,2,1,0:T(2,128)(2,1)S(1)} %get-tuple-element.82), channel_id=1, source_target_pairs={{8,0},{16,8},{24,16},{0,24},{9,1},{17,9},{25,17},{1,25},{10,2},{18... | collective-permute-start | bytes 24584 | tf_op jit(solution)/shard_map/ppermute | solution.py:18
  108.7 1.6 collective-permute-done.8
  110.4 2.6 %collective-permute-start.11 = (bf16[18,1,2,128]{3,2,1,0:T(2,128)(2,1)S(1)}, bf16[18,1,2,128]{3,2,1,0:T(2,128)(2,1)S(1)}, u32[]{:S(2)}, u32[]{:S(2)}) collective-permute-start(bf16[18,1,2,128]{3,2,1,0:T(2,128)(2,1)S(1)} %get-tuple-element.78), channel_id=1, source_target_pairs={{1,0},{2,1},{3,2},{4,3},{5,4},{6,5},{7,6},{0,7},{9,8},{10,9},{11,1... | collective-permute-start | bytes 27656 | tf_op jit(solution)/shard_map/ppermute | solution.py:18
  113.0 1.3 collective-permute-done.10
  117.1 3.9 %collective-permute-start.13 = (bf16[1,16,2,128]{3,2,1,0:T(2,128)(2,1)S(1)}, bf16[1,16,2,128]{3,2,1,0:T(2,128)(2,1)S(1)}, u32[]{:S(2)}, u32[]{:S(2)}) collective-permute-start(bf16[1,16,2,128]{3,2,1,0:T(2,128)(2,1)S(1)} %bitcast.376), channel_id=1, source_target_pairs={{8,0},{16,8},{24,16},{0,24},{9,1},{17,9},{25,17},{1,25},{10,2},{18... | collective-permute-start | bytes 24584 | tf_op jit(solution)/shard_map/ppermute | solution.py:18
  121.0 1.4 collective-permute-done.13
  122.3 4.1 %collective-permute-done.12 = bf16[1,16,2,128]{3,2,1,0:T(2,128)(2,1)S(1)} collective-permute-done((bf16[1,16,2,128]{3,2,1,0:T(2,128)(2,1)S(1)}, bf16[1,16,2,128]{3,2,1,0:T(2,128)(2,1)S(1)}, u32[]{:S(2)}, u32[]{:S(2)}) %collective-permute-start.12) | collective-permute-done | bytes 8224 | tf_op jit(solution)/shard_map/ppermute | solution.py:17
  126.5 2.6 %collective-permute-start.15 = (bf16[18,1,2,128]{3,2,1,0:T(2,128)(2,1)S(1)}, bf16[18,1,2,128]{3,2,1,0:T(2,128)(2,1)S(1)}, u32[]{:S(2)}, u32[]{:S(2)}) collective-permute-start(bf16[18,1,2,128]{3,2,1,0:T(2,128)(2,1)S(1)} %get-tuple-element.76), channel_id=1, source_target_pairs={{1,0},{2,1},{3,2},{4,3},{5,4},{6,5},{7,6},{0,7},{9,8},{10,9},{11,1... | collective-permute-start | bytes 27656 | tf_op jit(solution)/shard_map/ppermute | solution.py:18
  129.2 1.3 collective-permute-done.14
  133.9 3.8 %collective-permute-start.17 = (bf16[1,32,2,256]{3,2,1,0:T(2,128)(2,1)S(1)}, bf16[1,32,2,256]{3,2,1,0:T(2,128)(2,1)S(1)}, u32[]{:S(2)}, u32[]{:S(2)}) collective-permute-start(bf16[1,32,2,256]{3,2,1,0:T(2,128)(2,1)S(1)} %get-tuple-element.17), channel_id=1, source_target_pairs={{8,0},{16,8},{24,16},{0,24},{9,1},{17,9},{25,17},{1,25},{10,2},{18... | collective-permute-start | bytes 98312 | tf_op jit(solution)/shard_map/ppermute | solution.py:18
  137.7 1.9 collective-permute-done.16
  139.7 2.6 %collective-permute-start.19 = (bf16[34,1,2,256]{3,2,1,0:T(2,128)(2,1)S(1)}, bf16[34,1,2,256]{3,2,1,0:T(2,128)(2,1)S(1)}, u32[]{:S(2)}, u32[]{:S(2)}) collective-permute-start(bf16[34,1,2,256]{3,2,1,0:T(2,128)(2,1)S(1)} %get-tuple-element.15), channel_id=1, source_target_pairs={{1,0},{2,1},{3,2},{4,3},{5,4},{6,5},{7,6},{0,7},{9,8},{10,9},{11,1... | collective-permute-start | bytes 104456 | tf_op jit(solution)/shard_map/ppermute | solution.py:18
  142.4 1.6 collective-permute-done.18
  144.0 5.8 %broadcast_select_fusion = bf16[34,34,2,256]{3,2,1,0:T(2,128)(2,1)S(1)} fusion(pred[34]{0:T(512)(128)(4,1)S(1)} %compare_and_fusion.2, bf16[34,1,2,256]{3,2,1,0:T(2,128)(2,1)S(1)} %collective-permute-done.19, bf16[1,32,2,256]{3,2,1,0:T(2,128)(2,1)S(1)} %collective-permute-done.17, bf16[32,32,2,128]{3,2,1,0:T(2,128)(2,1)S(1)} %bitcast.305, ...), kind=kLoop, calls=%fused_computation.34 | loop fusion | flops 7694336 | bytes 2367522 | tf_op jit(solution)/shard_map/jit(_where)/select_n | solution.py:46
  149.8 10.8 %fusion.117 = (bf16[32,32,2,256]{3,2,1,0:T(2,128)(2,1)S(1)}, bf16[32,32,2,256]{3,2,1,0:T(2,128)(2,1)S(1)}, bf16[32,32,2,256]{3,2,1,0:T(2,128)(2,1)S(1)}, bf16[32...) fusion(bf16[34,34,2,256]{3,2,1,0:T(2,128)(2,1)S(1)} %broadcast_, ...), kind=kLoop, calls=%fused_computation.215 | loop fusion | bytes 18874368 | tf_op jit(solution)/shard_map/slice | solution.py:32
  160.5 1.2 reshape.318
  162.6 1.5 reshape.315
  164.1 2.2 %reshape.314 = bf16[2048,256]{1,0:T(8,128)(2,1)} reshape(bf16[32,32,2,256]{3,2,1,0:T(2,128)(2,1)} %get-tuple-element.9) | data formatting | bytes 2097152 | tf_op jit(solution)/shard_map/reshape | solution.py:32
  166.3 2.3 %reshape.313 = bf16[2048,256]{1,0:T(8,128)(2,1)} reshape(bf16[32,32,2,256]{3,2,1,0:T(2,128)(2,1)} %get-tuple-element.10) | data formatting | bytes 2097152 | tf_op jit(solution)/shard_map/reshape | solution.py:32
  168.6 2.3 %reshape.312 = bf16[2048,256]{1,0:T(8,128)(2,1)} reshape(bf16[32,32,2,256]{3,2,1,0:T(2,128)(2,1)} %get-tuple-element.11) | data formatting | bytes 2097152 | tf_op jit(solution)/shard_map/reshape | solution.py:32
  170.9 2.2 %reshape.311 = bf16[2048,256]{1,0:T(8,128)(2,1)} reshape(bf16[32,32,2,256]{3,2,1,0:T(2,128)(2,1)} %get-tuple-element.12) | data formatting | bytes 2097152 | tf_op jit(solution)/shard_map/reshape | solution.py:32
  173.1 2.3 %reshape.310 = bf16[2048,256]{1,0:T(8,128)(2,1)} reshape(bf16[32,32,2,256]{3,2,1,0:T(2,128)(2,1)} %get-tuple-element.13) | data formatting | bytes 2097152 | tf_op jit(solution)/shard_map/reshape | solution.py:32
  175.4 1.8 fusion.10
  183.8 3.9 %collective-permute-start.21 = (bf16[1,32,2,128]{3,2,1,0:T(2,128)(2,1)S(1)}, bf16[1,32,2,128]{3,2,1,0:T(2,128)(2,1)S(1)}, u32[]{:S(2)}, u32[]{:S(2)}) collective-permute-start(bf16[1,32,2,128]{3,2,1,0:T(2,128)(2,1)S(1)} %bitcast.374), channel_id=1, source_target_pairs={{8,0},{16,8},{24,16},{0,24},{9,1},{17,9},{25,17},{1,25},{10,2},{18... | collective-permute-start | bytes 49160 | tf_op jit(solution)/shard_map/ppermute | solution.py:18
  187.7 1.4 collective-permute-done.21
  189.1 4.1 %collective-permute-done.20 = bf16[1,32,2,128]{3,2,1,0:T(2,128)(2,1)S(1)} collective-permute-done((bf16[1,32,2,128]{3,2,1,0:T(2,128)(2,1)S(1)}, bf16[1,32,2,128]{3,2,1,0:T(2,128)(2,1)S(1)}, u32[]{:S(2)}, u32[]{:S(2)}) %collective-permute-start.20) | collective-permute-done | bytes 16416 | tf_op jit(solution)/shard_map/ppermute | solution.py:17
  193.4 2.6 %collective-permute-start.23 = (bf16[34,1,2,128]{3,2,1,0:T(2,128)(2,1)S(1)}, bf16[34,1,2,128]{3,2,1,0:T(2,128)(2,1)S(1)}, u32[]{:S(2)}, u32[]{:S(2)}) collective-permute-start(bf16[34,1,2,128]{3,2,1,0:T(2,128)(2,1)S(1)} %get-tuple-element.46), channel_id=1, source_target_pairs={{1,0},{2,1},{3,2},{4,3},{5,4},{6,5},{7,6},{0,7},{9,8},{10,9},{11,1... | collective-permute-start | bytes 52232 | tf_op jit(solution)/shard_map/ppermute | solution.py:18
  196.0 1.4 collective-permute-done.22
  197.5 1.7 broadcast_select_fusion.2
  199.2 5.2 %fusion.118 = (bf16[32,32,2,128]{3,2,1,0:T(2,128)(2,1)S(1)}, bf16[32,32,2,128]{3,2,1,0:T(2,128)(2,1)S(1)}, bf16[32,32,2,128]{3,2,1,0:T(2,128)(2,1)S(1)}, bf16[32...) fusion(bf16[34,34,2,128]{3,2,1,0:T(2,128)(2,1)S(1)} %broadcast_, ...), kind=kLoop, calls=%fused_computation.216 | loop fusion | bytes 9437184 | tf_op jit(solution)/shard_map/slice | solution.py:32
  207.5 1.3 copy.23
  (146 shorter events, 30.2 us)
Async XLA Ops:
  6.5 200.6 %copy-start = (bf16[128,64]{0,1:T(8,128)(2,1)S(1)}, bf16[128,64]{0,1:T(8,128)(2,1)}, u32[]{:S(2)}) copy-start(bf16[128,64]{0,1:T(8,128)(2,1)} %param.21) | copy-start | bytes 49156
  6.5 33.3 %all-gather.2.cloned.1.call-start = ((), (), s32[]{:S(2)}) async-start(), calls=%async_computation | async-start | bytes 2359296 | tf_op jit(solution)/shard_map/all_gather | solution.py:72
  61.5 5.7 %collective-permute-start = (bf16[1,32,2,64]{3,2,1,0:T(2,128)(2,1)S(1)}, bf16[1,32,2,64]{3,2,1,0:T(2,128)(2,1)S(1)}, u32[]{:S(2)}, u32[]{:S(2)}) collective-permute-start(bf16[1,32,2,64]{3,2,1,0:T(2,128)(2,1)S(1)} %slice.421), channel_id=1, source_target_pairs={{0,8},{8,16},{16,24},{24,0},{1,9},{9,17},{17,25},{25,1},{2,10},{10... | collective-permute-start | bytes 24584 | tf_op jit(solution)/shard_map/ppermute | solution.py:17
  63.4 4.4 %collective-permute-start.1 = (bf16[1,32,2,64]{3,2,1,0:T(2,128)(2,1)S(1)}, bf16[1,32,2,64]{3,2,1,0:T(2,128)(2,1)S(1)}, u32[]{:S(2)}, u32[]{:S(2)}) collective-permute-start(bf16[1,32,2,64]{3,2,1,0:T(2,128)(2,1)S(1)} %slice.423), channel_id=1, source_target_pairs={{8,0},{16,8},{24,16},{0,24},{9,1},{17,9},{25,17},{1,25},{10,2},{18... | collective-permute-start | bytes 24584 | tf_op jit(solution)/shard_map/ppermute | solution.py:18
  67.9 4.1 %collective-permute-start.2 = (bf16[34,1,2,64]{3,2,1,0:T(2,128)(2,1)S(1)}, bf16[34,1,2,64]{3,2,1,0:T(2,128)(2,1)S(1)}, u32[]{:S(2)}, u32[]{:S(2)}) collective-permute-start(bf16[34,1,2,64]{3,2,1,0:T(2,128)(2,1)S(1)} %get-tuple-element.49), channel_id=1, source_target_pairs={{0,1},{1,2},{2,3},{3,4},{4,5},{5,6},{6,7},{7,0},{8,9},{9,10},{10,1... | collective-permute-start | bytes 26120 | tf_op jit(solution)/shard_map/ppermute | solution.py:17
  67.9 4.1 %collective-permute-start.3 = (bf16[34,1,2,64]{3,2,1,0:T(2,128)(2,1)S(1)}, bf16[34,1,2,64]{3,2,1,0:T(2,128)(2,1)S(1)}, u32[]{:S(2)}, u32[]{:S(2)}) collective-permute-start(bf16[34,1,2,64]{3,2,1,0:T(2,128)(2,1)S(1)} %get-tuple-element.50), channel_id=1, source_target_pairs={{1,0},{2,1},{3,2},{4,3},{5,4},{6,5},{7,6},{0,7},{9,8},{10,9},{11,1... | collective-permute-start | bytes 26120 | tf_op jit(solution)/shard_map/ppermute | solution.py:18
  73.1 5.3 %copy-start.11 = (bf16[3,3,64,128]{3,2,1,0:T(8,128)(2,1)S(1)}, bf16[3,3,64,128]{3,2,1,0:T(8,128)(2,1)}, u32[]{:S(2)}) copy-start(bf16[3,3,64,128]{3,2,1,0:T(8,128)(2,1)} %param.15) | copy-start | bytes 442372
  81.0 4.9 %collective-permute-start.5 = (bf16[1,32,2,128]{3,2,1,0:T(2,128)(2,1)S(1)}, bf16[1,32,2,128]{3,2,1,0:T(2,128)(2,1)S(1)}, u32[]{:S(2)}, u32[]{:S(2)}) collective-permute-start(bf16[1,32,2,128]{3,2,1,0:T(2,128)(2,1)S(1)} %bitcast.373), channel_id=1, source_target_pairs={{8,0},{16,8},{24,16},{0,24},{9,1},{17,9},{25,17},{1,25},{10,2},{18... | collective-permute-start | bytes 49160 | tf_op jit(solution)/shard_map/ppermute | solution.py:18
  84.5 5.5 %collective-permute-start.4 = (bf16[1,32,2,128]{3,2,1,0:T(2,128)(2,1)S(1)}, bf16[1,32,2,128]{3,2,1,0:T(2,128)(2,1)S(1)}, u32[]{:S(2)}, u32[]{:S(2)}) collective-permute-start(bf16[1,32,2,128]{3,2,1,0:T(2,128)(2,1)S(1)} %bitcast.371), channel_id=1, source_target_pairs={{0,8},{8,16},{16,24},{24,0},{1,9},{9,17},{17,25},{25,1},{2,10},{10... | collective-permute-start | bytes 49160 | tf_op jit(solution)/shard_map/ppermute | solution.py:17
  90.1 4.3 %collective-permute-start.6 = (bf16[34,1,2,128]{3,2,1,0:T(2,128)(2,1)S(1)}, bf16[34,1,2,128]{3,2,1,0:T(2,128)(2,1)S(1)}, u32[]{:S(2)}, u32[]{:S(2)}) collective-permute-start(bf16[34,1,2,128]{3,2,1,0:T(2,128)(2,1)S(1)} %get-tuple-element.47), channel_id=1, source_target_pairs={{0,1},{1,2},{2,3},{3,4},{4,5},{5,6},{6,7},{7,0},{8,9},{9,10},{10,1... | collective-permute-start | bytes 52232 | tf_op jit(solution)/shard_map/ppermute | solution.py:17
  90.2 4.2 %collective-permute-start.7 = (bf16[34,1,2,128]{3,2,1,0:T(2,128)(2,1)S(1)}, bf16[34,1,2,128]{3,2,1,0:T(2,128)(2,1)S(1)}, u32[]{:S(2)}, u32[]{:S(2)}) collective-permute-start(bf16[34,1,2,128]{3,2,1,0:T(2,128)(2,1)S(1)} %get-tuple-element.48), channel_id=1, source_target_pairs={{1,0},{2,1},{3,2},{4,3},{5,4},{6,5},{7,6},{0,7},{9,8},{10,9},{11,1... | collective-permute-start | bytes 52232 | tf_op jit(solution)/shard_map/ppermute | solution.py:18
  96.1 5.3 %copy-start.9 = (bf16[3,3,128,128]{3,2,1,0:T(8,128)(2,1)S(1)}, bf16[3,3,128,128]{3,2,1,0:T(8,128)(2,1)}, u32[]{:S(2)}) copy-start(bf16[3,3,128,128]{3,2,1,0:T(8,128)(2,1)} %param.16) | copy-start | bytes 884740
  104.1 11.4 %copy-start.7 = (bf16[3,3,128,128]{3,2,1,0:T(8,128)(2,1)S(1)}, bf16[3,3,128,128]{3,2,1,0:T(8,128)(2,1)}, u32[]{:S(2)}) copy-start(bf16[3,3,128,128]{3,2,1,0:T(8,128)(2,1)} %param.17) | copy-start | bytes 884740
  104.8 5.5 %collective-permute-start.8 = (bf16[1,16,2,128]{3,2,1,0:T(2,128)(2,1)S(1)}, bf16[1,16,2,128]{3,2,1,0:T(2,128)(2,1)S(1)}, u32[]{:S(2)}, u32[]{:S(2)}) collective-permute-start(bf16[1,16,2,128]{3,2,1,0:T(2,128)(2,1)S(1)} %get-tuple-element.81), channel_id=1, source_target_pairs={{0,8},{8,16},{16,24},{24,0},{1,9},{9,17},{17,25},{25,1},{2,10},{10... | collective-permute-start | bytes 24584 | tf_op jit(solution)/shard_map/ppermute | solution.py:17
  104.9 5.4 %collective-permute-start.9 = (bf16[1,16,2,128]{3,2,1,0:T(2,128)(2,1)S(1)}, bf16[1,16,2,128]{3,2,1,0:T(2,128)(2,1)S(1)}, u32[]{:S(2)}, u32[]{:S(2)}) collective-permute-start(bf16[1,16,2,128]{3,2,1,0:T(2,128)(2,1)S(1)} %get-tuple-element.82), channel_id=1, source_target_pairs={{8,0},{16,8},{24,16},{0,24},{9,1},{17,9},{25,17},{1,25},{10,2},{18... | collective-permute-start | bytes 24584 | tf_op jit(solution)/shard_map/ppermute | solution.py:18
  110.3 4.0 %collective-permute-start.10 = (bf16[18,1,2,128]{3,2,1,0:T(2,128)(2,1)S(1)}, bf16[18,1,2,128]{3,2,1,0:T(2,128)(2,1)S(1)}, u32[]{:S(2)}, u32[]{:S(2)}) collective-permute-start(bf16[18,1,2,128]{3,2,1,0:T(2,128)(2,1)S(1)} %get-tuple-element.77), channel_id=1, source_target_pairs={{0,1},{1,2},{2,3},{3,4},{4,5},{5,6},{6,7},{7,0},{8,9},{9,10},{10,1... | collective-permute-start | bytes 27656 | tf_op jit(solution)/shard_map/ppermute | solution.py:17
  110.4 4.0 %collective-permute-start.11 = (bf16[18,1,2,128]{3,2,1,0:T(2,128)(2,1)S(1)}, bf16[18,1,2,128]{3,2,1,0:T(2,128)(2,1)S(1)}, u32[]{:S(2)}, u32[]{:S(2)}) collective-permute-start(bf16[18,1,2,128]{3,2,1,0:T(2,128)(2,1)S(1)} %get-tuple-element.78), channel_id=1, source_target_pairs={{1,0},{2,1},{3,2},{4,3},{5,4},{6,5},{7,6},{0,7},{9,8},{10,9},{11,1... | collective-permute-start | bytes 27656 | tf_op jit(solution)/shard_map/ppermute | solution.py:18
  116.9 14.8 %copy-start.8 = (bf16[3,3,128,128]{3,2,1,0:T(8,128)(2,1)S(1)}, bf16[3,3,128,128]{3,2,1,0:T(8,128)(2,1)}, u32[]{:S(2)}) copy-start(bf16[3,3,128,128]{3,2,1,0:T(8,128)(2,1)} %param.18) | copy-start | bytes 884740
  117.1 5.2 %collective-permute-start.13 = (bf16[1,16,2,128]{3,2,1,0:T(2,128)(2,1)S(1)}, bf16[1,16,2,128]{3,2,1,0:T(2,128)(2,1)S(1)}, u32[]{:S(2)}, u32[]{:S(2)}) collective-permute-start(bf16[1,16,2,128]{3,2,1,0:T(2,128)(2,1)S(1)} %bitcast.376), channel_id=1, source_target_pairs={{8,0},{16,8},{24,16},{0,24},{9,1},{17,9},{25,17},{1,25},{10,2},{18... | collective-permute-start | bytes 24584 | tf_op jit(solution)/shard_map/ppermute | solution.py:18
  121.0 5.4 %collective-permute-start.12 = (bf16[1,16,2,128]{3,2,1,0:T(2,128)(2,1)S(1)}, bf16[1,16,2,128]{3,2,1,0:T(2,128)(2,1)S(1)}, u32[]{:S(2)}, u32[]{:S(2)}) collective-permute-start(bf16[1,16,2,128]{3,2,1,0:T(2,128)(2,1)S(1)} %bitcast.375), channel_id=1, source_target_pairs={{0,8},{8,16},{16,24},{24,0},{1,9},{9,17},{17,25},{25,1},{2,10},{10... | collective-permute-start | bytes 24584 | tf_op jit(solution)/shard_map/ppermute | solution.py:17
  126.5 4.0 %collective-permute-start.14 = (bf16[18,1,2,128]{3,2,1,0:T(2,128)(2,1)S(1)}, bf16[18,1,2,128]{3,2,1,0:T(2,128)(2,1)S(1)}, u32[]{:S(2)}, u32[]{:S(2)}) collective-permute-start(bf16[18,1,2,128]{3,2,1,0:T(2,128)(2,1)S(1)} %get-tuple-element.75), channel_id=1, source_target_pairs={{0,1},{1,2},{2,3},{3,4},{4,5},{5,6},{6,7},{7,0},{8,9},{9,10},{10,1... | collective-permute-start | bytes 27656 | tf_op jit(solution)/shard_map/ppermute | solution.py:17
  126.5 4.0 %collective-permute-start.15 = (bf16[18,1,2,128]{3,2,1,0:T(2,128)(2,1)S(1)}, bf16[18,1,2,128]{3,2,1,0:T(2,128)(2,1)S(1)}, u32[]{:S(2)}, u32[]{:S(2)}) collective-permute-start(bf16[18,1,2,128]{3,2,1,0:T(2,128)(2,1)S(1)} %get-tuple-element.76), channel_id=1, source_target_pairs={{1,0},{2,1},{3,2},{4,3},{5,4},{6,5},{7,6},{0,7},{9,8},{10,9},{11,1... | collective-permute-start | bytes 27656 | tf_op jit(solution)/shard_map/ppermute | solution.py:18
  133.8 5.8 %collective-permute-start.16 = (bf16[1,32,2,256]{3,2,1,0:T(2,128)(2,1)S(1)}, bf16[1,32,2,256]{3,2,1,0:T(2,128)(2,1)S(1)}, u32[]{:S(2)}, u32[]{:S(2)}) collective-permute-start(bf16[1,32,2,256]{3,2,1,0:T(2,128)(2,1)S(1)} %get-tuple-element.16), channel_id=1, source_target_pairs={{0,8},{8,16},{16,24},{24,0},{1,9},{9,17},{17,25},{25,1},{2,10},{10... | collective-permute-start | bytes 98312 | tf_op jit(solution)/shard_map/ppermute | solution.py:17
  133.9 5.7 %collective-permute-start.17 = (bf16[1,32,2,256]{3,2,1,0:T(2,128)(2,1)S(1)}, bf16[1,32,2,256]{3,2,1,0:T(2,128)(2,1)S(1)}, u32[]{:S(2)}, u32[]{:S(2)}) collective-permute-start(bf16[1,32,2,256]{3,2,1,0:T(2,128)(2,1)S(1)} %get-tuple-element.17), channel_id=1, source_target_pairs={{8,0},{16,8},{24,16},{0,24},{9,1},{17,9},{25,17},{1,25},{10,2},{18... | collective-permute-start | bytes 98312 | tf_op jit(solution)/shard_map/ppermute | solution.py:18
  139.7 4.3 %collective-permute-start.18 = (bf16[34,1,2,256]{3,2,1,0:T(2,128)(2,1)S(1)}, bf16[34,1,2,256]{3,2,1,0:T(2,128)(2,1)S(1)}, u32[]{:S(2)}, u32[]{:S(2)}) collective-permute-start(bf16[34,1,2,256]{3,2,1,0:T(2,128)(2,1)S(1)} %get-tuple-element.14), channel_id=1, source_target_pairs={{0,1},{1,2},{2,3},{3,4},{4,5},{5,6},{6,7},{7,0},{8,9},{9,10},{10,1... | collective-permute-start | bytes 104456 | tf_op jit(solution)/shard_map/ppermute | solution.py:17
  139.7 4.2 %collective-permute-start.19 = (bf16[34,1,2,256]{3,2,1,0:T(2,128)(2,1)S(1)}, bf16[34,1,2,256]{3,2,1,0:T(2,128)(2,1)S(1)}, u32[]{:S(2)}, u32[]{:S(2)}) collective-permute-start(bf16[34,1,2,256]{3,2,1,0:T(2,128)(2,1)S(1)} %get-tuple-element.15), channel_id=1, source_target_pairs={{1,0},{2,1},{3,2},{4,3},{5,4},{6,5},{7,6},{0,7},{9,8},{10,9},{11,1... | collective-permute-start | bytes 104456 | tf_op jit(solution)/shard_map/ppermute | solution.py:18
  175.4 1.8 copy-start.4
  175.4 1.8 copy-start.6
  177.1 1.2 copy-start.3
  178.4 1.2 copy-start.2
  179.6 1.2 copy-start.1
  182.1 1.2 copy-start.5
  183.8 5.3 %collective-permute-start.21 = (bf16[1,32,2,128]{3,2,1,0:T(2,128)(2,1)S(1)}, bf16[1,32,2,128]{3,2,1,0:T(2,128)(2,1)S(1)}, u32[]{:S(2)}, u32[]{:S(2)}) collective-permute-start(bf16[1,32,2,128]{3,2,1,0:T(2,128)(2,1)S(1)} %bitcast.374), channel_id=1, source_target_pairs={{8,0},{16,8},{24,16},{0,24},{9,1},{17,9},{25,17},{1,25},{10,2},{18... | collective-permute-start | bytes 49160 | tf_op jit(solution)/shard_map/ppermute | solution.py:18
  187.7 5.5 %collective-permute-start.20 = (bf16[1,32,2,128]{3,2,1,0:T(2,128)(2,1)S(1)}, bf16[1,32,2,128]{3,2,1,0:T(2,128)(2,1)S(1)}, u32[]{:S(2)}, u32[]{:S(2)}) collective-permute-start(bf16[1,32,2,128]{3,2,1,0:T(2,128)(2,1)S(1)} %bitcast.372), channel_id=1, source_target_pairs={{0,8},{8,16},{16,24},{24,0},{1,9},{9,17},{17,25},{25,1},{2,10},{10... | collective-permute-start | bytes 49160 | tf_op jit(solution)/shard_map/ppermute | solution.py:17
  193.3 4.1 %collective-permute-start.22 = (bf16[34,1,2,128]{3,2,1,0:T(2,128)(2,1)S(1)}, bf16[34,1,2,128]{3,2,1,0:T(2,128)(2,1)S(1)}, u32[]{:S(2)}, u32[]{:S(2)}) collective-permute-start(bf16[34,1,2,128]{3,2,1,0:T(2,128)(2,1)S(1)} %get-tuple-element.45), channel_id=1, source_target_pairs={{0,1},{1,2},{2,3},{3,4},{4,5},{5,6},{6,7},{7,0},{8,9},{9,10},{10,1... | collective-permute-start | bytes 52232 | tf_op jit(solution)/shard_map/ppermute | solution.py:17
  193.4 4.1 %collective-permute-start.23 = (bf16[34,1,2,128]{3,2,1,0:T(2,128)(2,1)S(1)}, bf16[34,1,2,128]{3,2,1,0:T(2,128)(2,1)S(1)}, u32[]{:S(2)}, u32[]{:S(2)}) collective-permute-start(bf16[34,1,2,128]{3,2,1,0:T(2,128)(2,1)S(1)} %get-tuple-element.46), channel_id=1, source_target_pairs={{1,0},{2,1},{3,2},{4,3},{5,4},{6,5},{7,6},{0,7},{9,8},{10,9},{11,1... | collective-permute-start | bytes 52232 | tf_op jit(solution)/shard_map/ppermute | solution.py:18
  199.2 5.3 %copy-start.10 = (bf16[3,3,128,128]{3,2,1,0:T(8,128)(2,1)S(1)}, bf16[3,3,128,128]{3,2,1,0:T(8,128)(2,1)}, u32[]{:S(2)}) copy-start(bf16[3,3,128,128]{3,2,1,0:T(8,128)(2,1)} %param.20) | copy-start | bytes 884740
Sparse Core Ops, SparseCore 0:
  9.2 30.5 all-gather.1
where the time goes:
time: 216 us
  local copies, waits for them, and re-layouts  71.5 us (33%)
  waiting for transfers between devices  59.7 us (28%)
  starting transfers between devices  38.9 us (18%)
  matrix products  16.5 us (8%)
  other arithmetic  14.8 us (7%)
  between operations  14.2 us (7%)
    ppermute x12, starting transfers between devices, with_halo(): after = lax.ppermute(leading, axis, down)  37 us
    all_gather x1, waiting for transfers between devices, body(): lax.all_gather(source_tiles, 'col', axis=1, tiled=True).reshape(-1, columns)  28.5 us
    slice x6, local copies, waits for them, and re-layouts, conv_valid(): padded[row_step:row_step + height, col_step:col_step + width]  27.9 us
    ppermute x12, waiting for transfers between devices, with_halo(): before = lax.ppermute(last, axis, up)  26 us
    dot_general x54, matrix products, conv_valid(): jnp.dot(window, weight[row_step, col_step], preferred_element_type=jnp.fl...  16.3 us
    reshape x9, local copies, waits for them, and re-layouts, conv_valid(): padded[row_step:row_step + height, col_step:col_step + width]  14.8 us
    gather x1, local copies, waits for them, and re-layouts, body(): picked = buffer[stencil]  12.1 us
    select_n x6, other arithmetic, rim_clear(): jnp.where(inside[:, None, None, None], padded, jnp.zeros_like(padded))  10.9 us
  transfers between devices with their start and end apart: 25, of which 16 were waited for; matrix products, arithmetic and copies ran while one was open for 2% of the time, Pallas kernels for 0%

commit v1 on v0

v1 whole, which is shorter than its diff:
```python
import functools

import jax
import jax.numpy as jnp
from jax import lax
from jax.experimental import pallas as pl
from jax.experimental.pallas import tpu as pltpu
from jax.sharding import PartitionSpec as P

FIELDS = 64
CH = 128
HALO = 8


def silu(a):
    return a * (0.5 + 0.5 * jnp.tanh(0.5 * a))


def unet_kernel(
    tile_rows, tile_cols, p_ref, w_in, w_enc, w_m1, w_m2, w_d1, w_d2, w_out, out_ref,
    first, skip, pooled, middle, up, dec1, tmp, c_in, c_enc, c_m1, c_m2, c_d1u, c_d1s, c_d2, c_out,
):
    wide = tile_cols + 2 * HALO
    half = wide // 2
    row = lax.axis_index("row")
    at_top = row == 0
    at_bottom = row == lax.axis_size("row") - 1
    f32, bf16 = jnp.float32, jnp.bfloat16

    c_in[...] = jnp.zeros_like(c_in)
    c_out[...] = jnp.zeros_like(c_out)
    for b in range(2):
        c_out[b * CH : (b + 1) * CH, b * FIELDS : (b + 1) * FIELDS] = w_out[...]
    for dy in range(3):
        for dx in range(3):
            rows = slice(dy * CH, (dy + 1) * CH)
            cols = slice(dx * CH, (dx + 1) * CH)
            for b in range(2):
                c_in[b, dy * CH + b * FIELDS : dy * CH + (b + 1) * FIELDS, cols] = w_in[dy, dx]
            c_enc[rows, cols] = w_enc[dy, dx]
            c_m1[rows, cols] = w_m1[dy, dx]
            c_m2[rows, cols] = w_m2[dy, dx]
            c_d1u[rows, cols] = w_d1[dy, dx, :CH]
            c_d1s[rows, cols] = w_d1[dy, dx, CH:]
            c_d2[rows, cols] = w_d2[dy, dx]

    def conv(sources, width, chunk_rows, start):
        size = chunk_rows * width
        u = None
        for load, weight, offset in sources:
            windows = [
                load(pl.multiple_of(start + (offset + dy) * width, 8), size).astype(bf16)
                for dy in range(3)
            ]
            part = jnp.dot(
                jnp.concatenate(windows, axis=1), weight[...], preferred_element_type=f32
            )
            u = part if u is None else u + part
        return silu(
            u[:, CH : 2 * CH]
            + pltpu.roll(u[:, :CH], 1, 0)
            + pltpu.roll(u[:, 2 * CH :], size - 1, 0)
        )

    def per_chunk(height, chunk_rows, width, step):
        chunks = height // chunk_rows

        @pl.loop(0, 2 * chunks)
        def _(i):
            b = i // chunks
            start = pl.multiple_of((i % chunks) * (chunk_rows * width), 8)
            step(b, start)

    def clear(ref, depth, inner, width):
        @pl.when(at_top)
        def _():
            ref[:, : depth * width] = jnp.zeros((2, depth * width, CH), ref.dtype)

        @pl.when(at_bottom)
        def _():
            ref[:, (depth + inner) * width :] = jnp.zeros((2, depth * width, CH), ref.dtype)

    def reader(ref, b):
        return lambda start, size: ref[b, pl.ds(start, size), :]

    h_first = tile_rows + 14
    h_skip = tile_rows + 12
    h_pool = h_skip // 2
    h_mid = h_pool - 2
    h_coarse = h_mid - 2
    h_dec1 = tile_rows + 2

    def first_step(b, start):
        chunk = h_first // 2
        value = conv(
            [(lambda s, n: p_ref[pl.ds(s, n), :], c_in.at[b], 0)], wide, chunk, start
        )
        first[b, pl.ds(start, chunk * wide), :] = value.astype(bf16)

    per_chunk(h_first, h_first // 2, wide, first_step)
    clear(first, 7, tile_rows, wide)

    def skip_step(b, start):
        chunk = h_skip // 2
        value = conv([(reader(first, b), c_enc, 0)], wide, chunk, start)
        skip[b, pl.ds(start, chunk * wide), :] = value.astype(bf16)

    per_chunk(h_skip, h_skip // 2, wide, skip_step)
    clear(skip, 6, tile_rows, wide)

    @pl.loop(0, 2)
    def _(b):
        s = skip[b].astype(f32).reshape(h_pool, 2 * wide, CH)
        tmp[: h_pool * wide, :] = (s[:, :wide] + s[:, wide:]).reshape(h_pool * wide, CH)
        total = (
            tmp[pl.ds(0, h_pool * half, stride=2), :] + tmp[pl.ds(1, h_pool * half, stride=2), :]
        )
        pooled[b] = (total * 0.25).astype(bf16).astype(f32)

    def mid_step(b, start):
        value = conv([(reader(pooled, b), c_m1, 0)], half, h_mid, start)
        middle[b, pl.ds(start, h_mid * half), :] = value.astype(bf16).astype(f32)

    per_chunk(h_mid, h_mid, half, mid_step)
    clear(middle, 2, tile_rows // 2, half)

    @pl.loop(0, 2)
    def _(b):
        value = conv([(reader(middle, b), c_m2, 0)], half, h_coarse, 0)
        size = h_coarse * half
        tmp[pl.ds(0, size, stride=2), :] = value
        tmp[pl.ds(1, size, stride=2), :] = value
        v = tmp[: h_coarse * wide, :].astype(bf16).reshape(h_coarse, 1, wide, CH)
        up[b] = jnp.broadcast_to(v, (h_coarse, 2, wide, CH)).reshape(2 * h_coarse * wide, CH)

    clear(up, 2, tile_rows, wide)

    def dec1_step(b, start):
        chunk = h_dec1 // 2
        value = conv(
            [(reader(up, b), c_d1u, 0), (reader(skip, b), c_d1s, 4)], wide, chunk, start
        )
        dec1[b, pl.ds(start, chunk * wide), :] = value.astype(bf16)

    per_chunk(h_dec1, h_dec1 // 2, wide, dec1_step)
    clear(dec1, 1, tile_rows, wide)

    chunk = tile_rows // 2

    @pl.loop(0, 2)
    def _(i):
        start = pl.multiple_of(i * (chunk * wide), 8)
        both = []
        for b in range(2):
            value = conv([(reader(dec1, b), c_d2, 0)], wide, chunk, start)
            value = value.reshape(chunk, wide, CH)[:, HALO : HALO + tile_cols]
            both.append(value.reshape(chunk * tile_cols, CH).astype(bf16))
        result = jnp.dot(
            jnp.concatenate(both, axis=1), c_out[...], preferred_element_type=f32
        )
        place = pl.multiple_of(i * (chunk * tile_cols), 8)
        out_ref[pl.ds(place, chunk * tile_cols), :] = result.astype(bf16)


def unet(padded, tile_rows, tile_cols, weights):
    wide = tile_cols + 2 * HALO
    half = wide // 2
    f32, bf16 = jnp.float32, jnp.bfloat16
    square = pltpu.VMEM((3 * CH, 3 * CH), bf16)
    scratch = [
        pltpu.VMEM((2, (tile_rows + 14) * wide, CH), bf16),
        pltpu.VMEM((2, (tile_rows + 12) * wide, CH), bf16),
        pltpu.VMEM((2, (tile_rows // 2 + 6) * half, CH), f32),
        pltpu.VMEM((2, (tile_rows // 2 + 4) * half, CH), f32),
        pltpu.VMEM((2, (tile_rows + 4) * wide, CH), bf16),
        pltpu.VMEM((2, (tile_rows + 2) * wide, CH), bf16),
        pltpu.VMEM(((tile_rows // 2 + 6) * wide, CH), f32),
        pltpu.VMEM((2, 3 * CH, 3 * CH), bf16),
        square, square, square, square, square, square,
        pltpu.VMEM((2 * CH, 2 * FIELDS), bf16),
    ]
    return pl.pallas_call(
        functools.partial(unet_kernel, tile_rows, tile_cols),
        out_shape=jax.ShapeDtypeStruct((tile_rows * tile_cols, 2 * FIELDS), bf16),
        in_specs=[pl.BlockSpec(memory_space=pltpu.VMEM)] * 8,
        out_specs=pl.BlockSpec(memory_space=pltpu.VMEM),
        scratch_shapes=scratch,
        compiler_params=pltpu.CompilerParams(vmem_limit_bytes=44 * 1024 * 1024),
        cost_estimate=pl.CostEstimate(
            flops=6 * 10**9, bytes_accessed=4 * 10**6, transcendentals=2 * 10**6
        ),
    )(padded, *weights)


def with_halo(x, sides, width):
    for axis, dim in sides:
        devices, length = (lax.axis_size(axis), x.shape[dim])
        up = [(i, (i + 1) % devices) for i in range(devices)]
        down = [(j, i) for i, j in up]
        last = lax.slice_in_dim(x, length - width, length, axis=dim)
        leading = lax.slice_in_dim(x, 0, width, axis=dim)
        before = lax.ppermute(last, axis, up)
        after = lax.ppermute(leading, axis, down)
        x = jnp.concatenate([before, x, after], axis=dim)
    return x


def rim_clear(padded, depth, rows_dev):
    global_rows = (
        lax.axis_index("row") * rows_dev + jnp.arange(padded.shape[0], dtype=jnp.int32) - depth
    )
    inside = (global_rows >= 0) & (global_rows < lax.axis_size("row") * rows_dev)
    return jnp.where(inside[:, None, None], padded, jnp.zeros_like(padded))


def body(source_tiles, requests, stencil, regrid_weight, *weights):
    tile_rows = stencil.shape[0]
    tile_cols = stencil.shape[1]
    columns = source_tiles.shape[3]
    cells = source_tiles.shape[2]
    groups = requests.shape[2]
    capacity = requests.shape[3]
    wanted = requests.reshape(groups, capacity)
    global_ids = (jnp.arange(groups, dtype=jnp.int32)[:, None] * cells + wanted).reshape(-1)
    flattened = lax.all_gather(source_tiles, "col", axis=1, tiled=True).reshape(-1, columns)
    buffer = flattened[global_ids]
    picked = buffer[stencil]
    regridded = jnp.sum(picked.astype(jnp.float32) * regrid_weight[..., None], axis=2).astype(
        jnp.bfloat16
    )
    padded = rim_clear(with_halo(regridded, (("row", 0), ("col", 1)), HALO), HALO, tile_rows)
    result = unet(padded.reshape(-1, columns), tile_rows, tile_cols, weights)
    return result.reshape(tile_rows, tile_cols, 2, FIELDS)


def solution(mesh):
    placed = (P("row", "col", None, None),) * 2 + (P("row", "col", None),) * 2 + (P(),) * 7
    return jax.shard_map(
        body, mesh=mesh, in_specs=placed, out_specs=P("row", "col", None, None), check_vma=False
    )
```

time: 216 us -> 100 us (0.46)
  local copies, waits for them, and re-layouts: 71.5 us -> 22.6 us
  starting transfers between devices: 38.9 us -> 3.94 us
  waiting for transfers between devices: 59.7 us -> 41.1 us
  matrix products: 16.5 us -> 0 us
  Pallas kernels: 0 us -> 14.8 us
  other arithmetic: 14.8 us -> 3.8 us
    ppermute x12 -> x2, starting transfers between devices: 37 us -> 3.44 us  [with_halo(): after = lax.ppermute(leading, axis, down)]
    slice x8 -> x0, local copies, waits for them, and re-layouts: 28 us -> none  [the longest x6 27.9 us: conv_valid(): padded[row_step:row_step + height, col_step:col_step + width]]
    ppermute x12 -> x2, waiting for transfers between devices: 26 us -> 6.48 us  [with_halo(): before = lax.ppermute(last, axis, up)]
    dot_general x55 -> x0, matrix products: 16.5 us -> none  [the longest x54 16.3 us: conv_valid(): jnp.dot(window, weight[row_step, col_step], preferred_element_type=jnp.fl...]
    pallas_call x0 -> x1, Pallas kernels: none -> 14.8 us  [unet(): pl.pallas_call(functools.partial(unet_kernel, tile_rows, tile_cols), out_...]
    reshape x9 -> x1, local copies, waits for them, and re-layouts: 14.8 us -> 1.06 us  [body(): return result.reshape(tile_rows, tile_cols, 2, FIELDS)]
    select_n x8 -> x2, other arithmetic: 11.3 us -> 1.25 us  [the longest x1 1.23 us: rim_clear(): return jnp.where(inside[:, None, None], padded, jnp.zeros_like(padded))]
    unnamed x32 -> x21, local copies, waits for them, and re-layouts: 6.34 us -> 1.22 us
  transfers between devices with their start and end apart: 25 -> 5, of which waited for: 16 -> 5; matrix products, arithmetic and copies ran while one was open for 2% -> 3% of each run, Pallas kernels for 0% -> 0%
where the time goes in v1:
time: 100 us; the launch traced here: 99.9 us
  waiting for transfers between devices  41.1 us (41%)
  local copies, waits for them, and re-layouts  22.6 us (23%)
  Pallas kernels  14.8 us (15%)
  between operations  13.6 us (14%)
  starting transfers between devices  3.94 us (4%)
  other arithmetic  3.8 us (4%)
    all_gather x1, waiting for transfers between devices, body(): lax.all_gather(source_tiles, 'col', axis=1, tiled=True).reshape(-1, columns)  30.1 us
    pallas_call x1, Pallas kernels, unet(): pl.pallas_call(functools.partial(unet_kernel, tile_rows, tile_cols), out_...  14.8 us
    gather x1, local copies, waits for them, and re-layouts, body(): picked = buffer[stencil]  12.1 us
    gather x1, local copies, waits for them, and re-layouts, body(): buffer = flattened[global_ids]  7.46 us
    ppermute x2, waiting for transfers between devices, with_halo(): before = lax.ppermute(last, axis, up)  6.48 us
    ppermute x2, waiting for transfers between devices, with_halo(): after = lax.ppermute(leading, axis, down)  3.8 us
    ppermute x2, starting transfers between devices, with_halo(): after = lax.ppermute(leading, axis, down)  3.44 us
  transfers between devices with their start and end apart: 5, of which 5 were waited for; matrix products, arithmetic and copies ran while one was open for 3% of the time, Pallas kernels for 0%

profile of v1, /device:TPU:0, one launch (start us, length us, event | category | flops | bytes accessed | tf_op | source)
XLA Modules:
  0.0 99.9 jit_solution(6539455679975747630)
XLA Ops:
  6.5 0.0 copy-start.6
  6.5 0.0 all-gather.2.cloned.1.call-start
  6.5 0.7 all-gather.2.cloned.1.call-update
  7.3 0.1 broadcast_bitcast_fusion
  7.4 0.7 copy.22
  8.1 0.9 compare_select_fusion
  8.9 0.3 copy.18
  9.2 0.3 reshape.68
  9.5 0.0 copy-done.6
  9.5 0.3 copy.19
  9.8 30.1 %all-gather.2.cloned.1.call-done = bf16[1,8,1024,128]{3,2,0,1:T(8,128)(2,1)} async-done(((bf16[1,1,1024,128]{3,2,0,1:T(8,128)(2,1)}), bf16[1,8,1024,128]{3,2,0,1:T(8,128)(2,1)}) %all-gather.2.cloned.1.call-update) | async-done | bytes 2097168 | tf_op jit(solution)/shard_map/all_gather | solution.py:225
  39.9 7.5 %gather_fusion = bf16[2048,128]{1,0:T(8,128)(2,1)S(1)} fusion(bf16[8192,128]{1,0:T(8,128)(2,1)} %bitcast.16, s32[2048]{0:T(1024)S(1)} %broadcast_clamp_fusion.1), kind=kCustom, calls=%fused_computation | custom fusion | bytes 1056768 | tf_op jit(solution)/shard_map/gather | solution.py:226
  47.3 12.1 %gather_fusion.1 = bf16[4096,128]{1,0:T(8,128)(2,1)S(1)} fusion(bf16[2048,128]{1,0:T(8,128)(2,1)S(1)} %gather_fusion, s32[4096]{0:T(1024)S(1)} %broadcast_clamp_fusion), kind=kCustom, calls=%fused_computation.1 | custom fusion | bytes 2113536 | tf_op jit(solution)/shard_map/gather | solution.py:227
  59.5 0.0 copy-start.7
  59.5 1.6 %fusion = bf16[32,32,128]{2,1,0:T(8,128)(2,1)S(1)} fusion(bf16[32,32,4,128]{3,2,1,0:T(4,128)(2,1)S(1)} %bitcast.17, f32[32,32,4]{2,1,0:T(8,128)S(1)} %copy.19), kind=kLoop, calls=%fused_computation.3 | loop fusion | flops 1441792 | bytes 1327104 | tf_op jit(solution)/shard_map/reduce_sum | solution.py:228
  61.1 3.4 %collective-permute-start.1 = (bf16[8,32,128]{2,1,0:T(8,128)(2,1)S(1)}, bf16[8,32,128]{2,1,0:T(8,128)(2,1)S(1)}, u32[]{:S(2)}, u32[]{:S(2)}) collective-permute-start(bf16[8,32,128]{2,1,0:T(8,128)(2,1)S(1)} %get-tuple-element.8), channel_id=1, source_target_pairs={{8,0},{16,8},{24,16},{0,24},{9,1},{17,9},{25,17},{1,25},{10,2},{18... | collective-permute-start | bytes 196616 | tf_op jit(solution)/shard_map/ppermute | solution.py:203
  64.5 0.0 collective-permute-start
  64.5 2.4 %collective-permute-done.1 = bf16[8,32,128]{2,1,0:T(8,128)(2,1)S(1)} collective-permute-done((bf16[8,32,128]{2,1,0:T(8,128)(2,1)S(1)}, bf16[8,32,128]{2,1,0:T(8,128)(2,1)S(1)}, u32[]{:S(2)}, u32[]{:S(2)}) %collective-permute-start.1) | collective-permute-done | bytes 65568 | tf_op jit(solution)/shard_map/ppermute | solution.py:203
  66.9 3.6 %collective-permute-done = bf16[8,32,128]{2,1,0:T(8,128)(2,1)S(1)} collective-permute-done((bf16[8,32,128]{2,1,0:T(8,128)(2,1)S(1)}, bf16[8,32,128]{2,1,0:T(8,128)(2,1)S(1)}, u32[]{:S(2)}, u32[]{:S(2)}) %collective-permute-start) | collective-permute-done | bytes 65568 | tf_op jit(solution)/shard_map/ppermute | solution.py:202
  70.6 0.1 collective-permute-start.3
  70.6 0.5 collective-permute-start.2
  71.2 0.1 broadcast_in_dim.22
  71.2 0.1 broadcast_in_dim.23
  71.3 0.0 copy-done.7
  71.3 0.1 copy.20.w_out
  71.4 0.0 copy-start
  71.5 0.0 copy-start.1
  71.5 0.0 copy-start.2
  71.5 0.0 copy-start.3
  71.5 0.0 copy-start.4
  71.5 0.0 copy-start.5
  71.5 1.4 %collective-permute-done.3 = bf16[48,8,128]{2,1,0:T(8,128)(2,1)S(1)} collective-permute-done((bf16[48,8,128]{2,1,0:T(8,128)(2,1)S(1)}, bf16[48,8,128]{2,1,0:T(8,128)(2,1)S(1)}, u32[]{:S(2)}, u32[]{:S(2)}) %collective-permute-start.3) | collective-permute-done | bytes 98336 | tf_op jit(solution)/shard_map/ppermute | solution.py:203
  72.9 2.9 %collective-permute-done.2 = bf16[48,8,128]{2,1,0:T(8,128)(2,1)S(1)} collective-permute-done((bf16[48,8,128]{2,1,0:T(8,128)(2,1)S(1)}, bf16[48,8,128]{2,1,0:T(8,128)(2,1)S(1)}, u32[]{:S(2)}, u32[]{:S(2)}) %collective-permute-start.2) | collective-permute-done | bytes 98336 | tf_op jit(solution)/shard_map/ppermute | solution.py:202
  75.7 0.1 pad_maximum_fusion
  75.8 1.2 %bitcast_select_fusion.p_ref = bf16[2304,128]{1,0:T(8,128)(2,1)S(1)} fusion(bf16[48,48,128]{2,1,0:T(8,128)(2,1)S(1)} %pad_maximum_fusion, pred[2304]{0:T(1024)(128)(4,1)S(1)} %broadcast_in_dim.23), kind=kLoop, calls=%fused_computation.5 | loop fusion | flops 294912 | bytes 1181952 | tf_op jit(solution)/shard_map/jit(_where)/select_n | solution.py:213
  77.0 0.0 copy-done
  77.1 0.0 copy-done.1
  77.1 0.0 copy-done.2
  77.1 0.0 copy-done.3
  77.1 0.0 copy-done.4
  77.1 0.0 copy-done.5
  77.1 14.8 %shard_map.109 = bf16[1024,128]{1,0:T(8,128)(2,1)S(1)} custom-call(bf16[2304,128]{1,0:T(8,128)(2,1)S(1)} %bitcast_select_fusion.p_ref, bf16[3,3,64,128]{3,2,1,0:T(8,128)(2,1)S(1)} %copy-done.5, bf16[3,3,128,128]{3,2,1,0:T(8,128)(2,1)S(1)} %copy-done.1, bf16[3,3,128,128]{3,2,1,0:T(8,128)(2,1)S(1)} %copy-done.2, bf16[3,3,128,128]{3,2,1,0:T(8,128)(2,1)S(1)} %copy-done.3, ...), custom_call_target="tpu_custom_call" | custom-call | flops 6000000000 | bytes 4000000 | tf_op jit(solution)/shard_map/pallas_call | solution.py:182
  92.0 1.1 %reshape.57 = bf16[32,32,2,64]{3,2,1,0:T(2,128)(2,1)} reshape(bf16[1024,128]{1,0:T(8,128)(2,1)S(1)} %shard_map.109) | data formatting | bytes 524288 | tf_op jit(solution)/shard_map/reshape | solution.py:233
  (8 shorter events, 0.1 us)
Async XLA Ops:
  6.5 2.9 %copy-start.6 = (f32[32,32,4]{1,2,0:T(4,128)S(1)}, f32[32,32,4]{1,2,0:T(4,128)}, u32[]{:S(2)}) copy-start(f32[32,32,4]{1,2,0:T(4,128)} %param.14) | copy-start | bytes 49156
  6.5 33.3 %all-gather.2.cloned.1.call-start = ((), (), s32[]{:S(2)}) async-start(), calls=%async_computation | async-start | bytes 2359296 | tf_op jit(solution)/shard_map/all_gather | solution.py:225
  59.5 11.8 %copy-start.7 = (bf16[128,64]{0,1:T(8,128)(2,1)S(1)}, bf16[128,64]{0,1:T(8,128)(2,1)}, u32[]{:S(2)}) copy-start(bf16[128,64]{0,1:T(8,128)(2,1)} %param.21) | copy-start | bytes 49156
  61.1 5.8 %collective-permute-start.1 = (bf16[8,32,128]{2,1,0:T(8,128)(2,1)S(1)}, bf16[8,32,128]{2,1,0:T(8,128)(2,1)S(1)}, u32[]{:S(2)}, u32[]{:S(2)}) collective-permute-start(bf16[8,32,128]{2,1,0:T(8,128)(2,1)S(1)} %get-tuple-element.8), channel_id=1, source_target_pairs={{8,0},{16,8},{24,16},{0,24},{9,1},{17,9},{25,17},{1,25},{10,2},{18... | collective-permute-start | bytes 196616 | tf_op jit(solution)/shard_map/ppermute | solution.py:203
  64.5 6.1 %collective-permute-start = (bf16[8,32,128]{2,1,0:T(8,128)(2,1)S(1)}, bf16[8,32,128]{2,1,0:T(8,128)(2,1)S(1)}, u32[]{:S(2)}, u32[]{:S(2)}) collective-permute-start(bf16[8,32,128]{2,1,0:T(8,128)(2,1)S(1)} %get-tuple-element.7), channel_id=1, source_target_pairs={{0,8},{8,16},{16,24},{24,0},{1,9},{9,17},{17,25},{25,1},{2,10},{10... | collective-permute-start | bytes 196616 | tf_op jit(solution)/shard_map/ppermute | solution.py:202
  70.6 2.3 %collective-permute-start.3 = (bf16[48,8,128]{2,1,0:T(8,128)(2,1)S(1)}, bf16[48,8,128]{2,1,0:T(8,128)(2,1)S(1)}, u32[]{:S(2)}, u32[]{:S(2)}) collective-permute-start(bf16[48,8,128]{2,1,0:T(8,128)(2,1)S(1)} %get-tuple-element.6), channel_id=1, source_target_pairs={{1,0},{2,1},{3,2},{4,3},{5,4},{6,5},{7,6},{0,7},{9,8},{10,9},{11,1... | collective-permute-start | bytes 294920 | tf_op jit(solution)/shard_map/ppermute | solution.py:203
  70.6 5.1 %collective-permute-start.2 = (bf16[48,8,128]{2,1,0:T(8,128)(2,1)S(1)}, bf16[48,8,128]{2,1,0:T(8,128)(2,1)S(1)}, u32[]{:S(2)}, u32[]{:S(2)}) collective-permute-start(bf16[48,8,128]{2,1,0:T(8,128)(2,1)S(1)} %get-tuple-element.5), channel_id=1, source_target_pairs={{0,1},{1,2},{2,3},{3,4},{4,5},{5,6},{6,7},{7,0},{8,9},{9,10},{10,1... | collective-permute-start | bytes 294920 | tf_op jit(solution)/shard_map/ppermute | solution.py:202
  71.4 5.6 %copy-start = (bf16[3,3,256,128]{3,2,1,0:T(8,128)(2,1)S(1)}, bf16[3,3,256,128]{3,2,1,0:T(8,128)(2,1)}, u32[]{:S(2)}) copy-start(bf16[3,3,256,128]{3,2,1,0:T(8,128)(2,1)} %w_d1.1) | copy-start | bytes 1769476
  71.5 5.6 %copy-start.1 = (bf16[3,3,128,128]{3,2,1,0:T(8,128)(2,1)S(1)}, bf16[3,3,128,128]{3,2,1,0:T(8,128)(2,1)}, u32[]{:S(2)}) copy-start(bf16[3,3,128,128]{3,2,1,0:T(8,128)(2,1)} %w_enc.1) | copy-start | bytes 884740
  71.5 5.6 %copy-start.2 = (bf16[3,3,128,128]{3,2,1,0:T(8,128)(2,1)S(1)}, bf16[3,3,128,128]{3,2,1,0:T(8,128)(2,1)}, u32[]{:S(2)}) copy-start(bf16[3,3,128,128]{3,2,1,0:T(8,128)(2,1)} %w_m1.1) | copy-start | bytes 884740
  71.5 5.6 %copy-start.3 = (bf16[3,3,128,128]{3,2,1,0:T(8,128)(2,1)S(1)}, bf16[3,3,128,128]{3,2,1,0:T(8,128)(2,1)}, u32[]{:S(2)}) copy-start(bf16[3,3,128,128]{3,2,1,0:T(8,128)(2,1)} %w_m2.1) | copy-start | bytes 884740
  71.5 5.6 %copy-start.4 = (bf16[3,3,128,128]{3,2,1,0:T(8,128)(2,1)S(1)}, bf16[3,3,128,128]{3,2,1,0:T(8,128)(2,1)}, u32[]{:S(2)}) copy-start(bf16[3,3,128,128]{3,2,1,0:T(8,128)(2,1)} %w_d2.1) | copy-start | bytes 884740
  71.5 5.6 %copy-start.5 = (bf16[3,3,64,128]{3,2,1,0:T(8,128)(2,1)S(1)}, bf16[3,3,64,128]{3,2,1,0:T(8,128)(2,1)}, u32[]{:S(2)}) copy-start(bf16[3,3,64,128]{3,2,1,0:T(8,128)(2,1)} %w_in.1) | copy-start | bytes 442372
Sparse Core Ops, SparseCore 0:
  9.2 30.5 all-gather.1

commit v2 on v1

--- a/solution.py
+++ b/solution.py
@@ -192,44 +192,248 @@
     )(padded, *weights)
 
 
-def with_halo(x, sides, width):
-    for axis, dim in sides:
-        devices, length = (lax.axis_size(axis), x.shape[dim])
-        up = [(i, (i + 1) % devices) for i in range(devices)]
-        down = [(j, i) for i, j in up]
-        last = lax.slice_in_dim(x, length - width, length, axis=dim)
-        leading = lax.slice_in_dim(x, 0, width, axis=dim)
-        before = lax.ppermute(last, axis, up)
-        after = lax.ppermute(leading, axis, down)
-        x = jnp.concatenate([before, x, after], axis=dim)
-    return x
-
-
-def rim_clear(padded, depth, rows_dev):
-    global_rows = (
-        lax.axis_index("row") * rows_dev + jnp.arange(padded.shape[0], dtype=jnp.int32) - depth
+MESH = pl.DeviceIdType.MESH
+
+
+def regrid_kernel(
+    tile_rows, tile_cols, src_ref, req_ref, sten_ref, wgt_ref, out_ref,
+    reqs, src_t, mix, outbox, inbox, acc, pad,
+    req_send, req_recv, box_send, box_recv, halo_send, halo_recv,
+):
+    f32, bf16 = jnp.float32, jnp.bfloat16
+    row, me = lax.axis_index("row"), lax.axis_index("col")
+    n_row, n = lax.axis_size("row"), lax.axis_size("col")
+    cap = req_ref.shape[1]
+    cells = src_ref.shape[0]
+    spots = tile_rows * tile_cols
+    has_up, has_down = row > 0, row < n_row - 1
+    blocks = tile_cols // HALO
+    edge = HALO * HALO
+    inner = tile_rows * HALO
+
+    barrier = pltpu.get_barrier_semaphore()
+
+    def greet(r, c):
+        pl.semaphore_signal(
+            barrier, inc=1, device_id=(r, lax.rem(c + n, n)), device_id_type=MESH
+        )
+
+    @pl.loop(1, n)
+    def _(step):
+        greet(row, me + step)
+
+    @pl.when(has_up)
+    def _():
+        for d in (-1, 0, 1):
+            greet(row - 1, me + d)
+
+    @pl.when(has_down)
+    def _():
+        for d in (-1, 0, 1):
+            greet(row + 1, me + d)
+
+    rows_beside = jnp.minimum(row, 1) + jnp.minimum(n_row - 1 - row, 1)
+    pl.semaphore_wait(barrier, n - 1 + 3 * rows_beside)
+
+    def ask(step, sender):
+        return pltpu.make_async_remote_copy(
+            src_ref=req_ref,
+            dst_ref=reqs.at[sender],
+            send_sem=req_send.at[step],
+            recv_sem=req_recv.at[sender],
+            device_id=(row, lax.rem(me + step, n)),
+            device_id_type=MESH,
+        )
+
+    @pl.loop(1, n)
+    def _(step):
+        ask(step, me).start()
+
+    reqs[me] = req_ref[...]
+    src_t[...] = src_ref[...].astype(f32).T.astype(bf16)
+
+    def mix_block(j):
+        slots = lax.broadcasted_iota(jnp.int32, (cap, spots), 0)
+        total = None
+        for k in range(sten_ref.shape[0]):
+            hit = slots == sten_ref[k : k + 1, :] - j * cap
+            part = jnp.where(hit, wgt_ref[k : k + 1, :], 0.0)
+            total = part if total is None else total + part
+        mix[j] = total.astype(bf16)
+
+    @pl.loop(0, n // 2)
+    def _(j):
+        mix_block(j)
+
+    def picked(dest):
+        ids = lax.broadcasted_iota(jnp.int32, (cells, cap), 0)
+        hot = jnp.where(ids == reqs[dest, pl.ds(me, 1), :], 1.0, 0.0).astype(bf16)
+        return jnp.dot(src_t[...], hot, preferred_element_type=f32).astype(bf16)
+
+    def post(step, sender):
+        return pltpu.make_async_remote_copy(
+            src_ref=outbox.at[step],
+            dst_ref=inbox.at[sender],
+            send_sem=box_send.at[step],
+            recv_sem=box_recv.at[sender],
+            device_id=(row, lax.rem(me + step, n)),
+            device_id_type=MESH,
+        )
+
+    @pl.loop(1, n)
+    def _(step):
+        dest = lax.rem(me + step, n)
+        ask(step, dest).wait_recv()
+        outbox[step] = picked(dest)
+        post(step, me).start()
+
+    inbox[me] = picked(me)
+
+    @pl.loop(n // 2, n)
+    def _(j):
+        mix_block(j)
+
+    acc[...] = jnp.dot(inbox[me], mix[me], preferred_element_type=f32)
+
+    @pl.loop(1, n)
+    def _(step):
+        sender = lax.rem(me - step + n, n)
+        post(step, sender).wait_recv()
+        acc[...] += jnp.dot(inbox[sender], mix[sender], preferred_element_type=f32)
+
+    grid = acc[...].T.reshape(tile_rows, blocks, HALO, 2 * FIELDS)
+    for xb in range(blocks):
+        pad[xb + 1, edge : edge + inner, :] = (
+            grid[:, xb].reshape(inner, 2 * FIELDS).astype(bf16)
+        )
+
+    @pl.when(jnp.logical_not(has_up))
+    def _():
+        pad[:, :edge] = jnp.zeros((blocks + 2, edge, 2 * FIELDS), bf16)
+
+    @pl.when(jnp.logical_not(has_down))
+    def _():
+        pad[:, edge + inner :] = jnp.zeros((blocks + 2, edge, 2 * FIELDS), bf16)
+
+    mid = slice(edge, edge + inner)
+    first, last = slice(edge, 2 * edge), slice(inner, inner + edge)
+    low, high = slice(0, edge), slice(edge + inner, 2 * edge + inner)
+    every = slice(1, blocks + 1)
+    left, right = slice(1, 2), slice(blocks, blocks + 1)
+    before, after = slice(0, 1), slice(blocks + 1, blocks + 2)
+    moves = [
+        (0, 1, (right, mid), (before, mid)),
+        (0, -1, (left, mid), (after, mid)),
+        (1, 0, (every, last), (every, low)),
+        (1, 1, (right, last), (before, low)),
+        (1, -1, (left, last), (after, low)),
+        (-1, 0, (every, first), (every, high)),
+        (-1, 1, (right, first), (before, high)),
+        (-1, -1, (left, first), (after, high)),
+    ]
+
+    def shift(i):
+        dr, dc, src, dst = moves[i]
+        return pltpu.make_async_remote_copy(
+            src_ref=pad.at[src[0], src[1]],
+            dst_ref=pad.at[dst[0], dst[1]],
+            send_sem=halo_send.at[i],
+            recv_sem=halo_recv.at[i],
+            device_id=(row + dr, lax.rem(me + dc + n, n)),
+            device_id_type=MESH,
+        )
+
+    @pl.when(has_down)
+    def _():
+        for i in (2, 3, 4):
+            shift(i).start()
+
+    @pl.when(has_up)
+    def _():
+        for i in (5, 6, 7):
+            shift(i).start()
+
+    for i in (0, 1):
+        shift(i).start()
+    for i in (0, 1):
+        shift(i).wait()
+
+    @pl.when(has_up)
+    def _():
+        for i in (2, 3, 4):
+            shift(i).wait_recv()
+
+    @pl.when(has_down)
+    def _():
+        for i in (5, 6, 7):
+            shift(i).wait_recv()
+
+    parts = [
+        pad[xb].astype(f32).reshape(tile_rows + 2 * HALO, HALO, 2 * FIELDS)
+        for xb in range(blocks + 2)
+    ]
+    out_ref[...] = jnp.concatenate(parts, axis=1).reshape(out_ref.shape).astype(bf16)
+
+    @pl.when(has_down)
+    def _():
+        for i in (2, 3, 4):
+            shift(i).wait_send()
+
+    @pl.when(has_up)
+    def _():
+        for i in (5, 6, 7):
+            shift(i).wait_send()
+
+    @pl.loop(1, n)
+    def _(step):
+        ask(step, me).wait_send()
+        post(step, me).wait_send()
+
+
+def regrid(source, wanted, stencil, weight, tile_rows, tile_cols):
+    f32, bf16 = jnp.float32, jnp.bfloat16
+    n, cap = wanted.shape
+    cells, columns = source.shape
+    spots = tile_rows * tile_cols
+    blocks = tile_cols // HALO
+    rows = tile_rows + 2 * HALO
+    dma = pltpu.SemaphoreType.DMA
+    return pl.pallas_call(
+        functools.partial(regrid_kernel, tile_rows, tile_cols),
+        out_shape=jax.ShapeDtypeStruct((rows * (tile_cols + 2 * HALO), columns), bf16),
+        in_specs=[pl.BlockSpec(memory_space=pltpu.VMEM)] * 4,
+        out_specs=pl.BlockSpec(memory_space=pltpu.VMEM),
+        scratch_shapes=[
+            pltpu.VMEM((n, n, cap), jnp.int32),
+            pltpu.VMEM((columns, cells), bf16),
+            pltpu.VMEM((n, cap, spots), bf16),
+            pltpu.VMEM((n, columns, cap), bf16),
+            pltpu.VMEM((n, columns, cap), bf16),
+            pltpu.VMEM((columns, spots), f32),
+            pltpu.VMEM((blocks + 2, rows * HALO, columns), bf16),
+            dma((n,)), dma((n,)), dma((n,)), dma((n,)), dma((8,)), dma((8,)),
+        ],
+        compiler_params=pltpu.CompilerParams(
+            collective_id=0, has_side_effects=True, vmem_limit_bytes=40 * 1024 * 1024
+        ),
+        cost_estimate=pl.CostEstimate(
+            flops=10**9, bytes_accessed=2 * 10**6, transcendentals=0
+        ),
+    )(source, wanted, stencil, weight)
+
+
+def body(source_tiles, requests, stencil, regrid_weight, *weights):
+    tile_rows, tile_cols, taps = stencil.shape
+    cells, columns = source_tiles.shape[2:]
+    padded = regrid(
+        source_tiles.reshape(cells, columns),
+        requests.reshape(requests.shape[2:]),
+        stencil.transpose(2, 0, 1).reshape(taps, -1),
+        regrid_weight.transpose(2, 0, 1).reshape(taps, -1),
+        tile_rows,
+        tile_cols,
     )
-    inside = (global_rows >= 0) & (global_rows < lax.axis_size("row") * rows_dev)
-    return jnp.where(inside[:, None, None], padded, jnp.zeros_like(padded))
-
-
-def body(source_tiles, requests, stencil, regrid_weight, *weights):
-    tile_rows = stencil.shape[0]
-    tile_cols = stencil.shape[1]
-    columns = source_tiles.shape[3]
-    cells = source_tiles.shape[2]
-    groups = requests.shape[2]
-    capacity = requests.shape[3]
-    wanted = requests.reshape(groups, capacity)
-    global_ids = (jnp.arange(groups, dtype=jnp.int32)[:, None] * cells + wanted).reshape(-1)
-    flattened = lax.all_gather(source_tiles, "col", axis=1, tiled=True).reshape(-1, columns)
-    buffer = flattened[global_ids]
-    picked = buffer[stencil]
-    regridded = jnp.sum(picked.astype(jnp.float32) * regrid_weight[..., None], axis=2).astype(
-        jnp.bfloat16
-    )
-    padded = rim_clear(with_halo(regridded, (("row", 0), ("col", 1)), HALO), HALO, tile_rows)
-    result = unet(padded.reshape(-1, columns), tile_rows, tile_cols, weights)
+    result = unet(padded, tile_rows, tile_cols, weights)
     return result.reshape(tile_rows, tile_cols, 2, FIELDS)
 
 

time: 100 us -> 41 us (0.41)
  waiting for transfers between devices: 41.1 us -> 0 us
  Pallas kernels: 14.8 us -> 36.2 us
  local copies, waits for them, and re-layouts: 22.6 us -> 4.44 us
  between operations: 13.6 us -> 0.1 us
  starting transfers between devices: 3.94 us -> 0 us
  other arithmetic: 3.8 us -> 0 us
    all_gather x1 -> x0, waiting for transfers between devices: 30.1 us -> none  [body(): lax.all_gather(source_tiles, 'col', axis=1, tiled=True).reshape(-1, columns)]
    pallas_call x0 -> x1, Pallas kernels: none -> 21.4 us  [regrid(): pl.pallas_call(functools.partial(regrid_kernel, tile_rows, tile_cols), ou...]
    gather x2 -> x0, local copies, waits for them, and re-layouts: 19.6 us -> none  [the longest x1 12.1 us: body(): picked = buffer[stencil]]
    ppermute x4 -> x0, waiting for transfers between devices: 10.3 us -> none  [the longest x2 6.48 us: with_halo(): before = lax.ppermute(last, axis, up)]
    ppermute x4 -> x0, starting transfers between devices: 3.94 us -> none  [the longest x2 3.44 us: with_halo(): after = lax.ppermute(leading, axis, down)]
    select_n x3 -> x0, other arithmetic: 2.11 us -> none  [the longest x1 1.23 us: rim_clear(): return jnp.where(inside[:, None, None], padded, jnp.zeros_like(padded))]
    transpose x0 -> x2, local copies, waits for them, and re-layouts: none -> 1.7 us  [the longest x1 0.86 us: body(): stencil.transpose(2, 0, 1).reshape(taps, -1)]
    reduce_sum x1 -> x0, other arithmetic: 1.6 us -> none  [body(): jnp.sum(picked.astype(jnp.float32) * regrid_weight[..., None], axis=2)]
  transfers between devices with their start and end apart: 5 -> 0, of which waited for: 5 -> 0; matrix products, arithmetic and copies ran while one was open for 3% -> 0% of each run, Pallas kernels for 0% -> 0%
where the time goes in v2:
time: 41 us; the launch traced here: 40.7 us
  Pallas kernels  36.2 us (88%)
  local copies, waits for them, and re-layouts  4.44 us (11%)
    pallas_call x1, Pallas kernels, regrid(): pl.pallas_call(functools.partial(regrid_kernel, tile_rows, tile_cols), ou...  21.4 us
    pallas_call x1, Pallas kernels, unet(): pl.pallas_call(functools.partial(unet_kernel, tile_rows, tile_cols), out_...  14.8 us
    unnamed x17, local copies, waits for them, and re-layouts  1.49 us
    reshape x1, local copies, waits for them, and re-layouts, body(): return result.reshape(tile_rows, tile_cols, 2, FIELDS)  1.06 us
    transpose x1, local copies, waits for them, and re-layouts, body(): stencil.transpose(2, 0, 1).reshape(taps, -1)  0.86 us
    transpose x1, local copies, waits for them, and re-layouts, body(): regrid_weight.transpose(2, 0, 1).reshape(taps, -1)  0.84 us

profile of v2, /device:TPU:0, one launch (start us, length us, event | category | flops | bytes accessed | tf_op | source)
XLA Modules:
  0.0 40.7 jit_solution(3524205290356222130)
XLA Ops:
  0.0 0.0 copy-start.5
  0.0 0.9 %copy.14.w_out = bf16[128,64]{1,0:T(8,128)(2,1)S(1)} copy(bf16[128,64]{0,1:T(8,128)(2,1)} %param.21) | data formatting | bytes 32768 | tf_op args[10]
  0.9 0.9 %copy.12 = s32[4,32,32]{2,1,0:T(8,128)S(1)} copy(s32[4,32,32]{2,0,1:T(4,128)} %bitcast.6) | data formatting | bytes 32768 | tf_op jit(solution)/shard_map/transpose | solution.py:431
  1.7 0.1 reshape.17.sten_ref
  1.8 0.8 %copy.13 = f32[4,32,32]{2,1,0:T(8,128)S(1)} copy(f32[4,32,32]{2,0,1:T(4,128)} %bitcast.7) | data formatting | bytes 32768 | tf_op jit(solution)/shard_map/transpose | solution.py:432
  2.7 0.0 copy-start.7
  2.7 0.1 reshape.18.wgt_ref
  2.8 0.0 copy-done.5
  2.8 0.6 %copy-done.7 = s32[1,1,8,256]{3,2,1,0:T(8,128)S(1)} copy-done((s32[1,1,8,256]{3,2,1,0:T(8,128)S(1)}, s32[1,1,8,256]{3,2,1,0:T(8,128)}, u32[]{:S(2)}) %copy-start.7) | copy-done | bytes 8216
  3.4 0.0 copy-start
  3.4 0.0 copy-start.1
  3.4 0.0 copy-start.2
  3.4 0.0 copy-start.3
  3.4 0.0 copy-start.4
  3.4 0.0 copy-start.6
  3.4 21.4 %shard_map.109.p_ref = bf16[2304,128]{1,0:T(8,128)(2,1)S(1)} custom-call(bf16[1024,128]{1,0:T(8,128)(2,1)S(1)} %bitcast.4, s32[8,256]{1,0:T(8,128)S(1)} %bitcast.5, s32[4,1024]{1,0:T(4,128)S(1)} %reshape.17.sten_ref, f32[4,1024]{1,0:T(4,128)S(1)} %reshape.18.wgt_ref), custom_call_target="tpu_custom_call" | custom-call | flops 1000000000 | bytes 2000000 | tf_op jit(solution)/shard_map/pallas_call | solution.py:401
  24.8 0.0 copy-done
  24.8 0.0 copy-done.1
  24.8 0.0 copy-done.2
  24.8 0.0 copy-done.3
  24.8 0.0 copy-done.4
  24.8 0.0 copy-done.6
  24.8 14.8 %shard_map.110 = bf16[1024,128]{1,0:T(8,128)(2,1)S(1)} custom-call(bf16[2304,128]{1,0:T(8,128)(2,1)S(1)} %shard_map.109.p_ref, bf16[3,3,64,128]{3,2,1,0:T(8,128)(2,1)S(1)} %copy-done.6, bf16[3,3,128,128]{3,2,1,0:T(8,128)(2,1)S(1)} %copy-done.1, bf16[3,3,128,128]{3,2,1,0:T(8,128)(2,1)S(1)} %copy-done.2, bf16[3,3,128,128]{3,2,1,0:T(8,128)(2,1)S(1)} %copy-done.3, ...), custom_call_target="tpu_custom_call" | custom-call | flops 6000000000 | bytes 4000000 | tf_op jit(solution)/shard_map/pallas_call | solution.py:182
  39.7 1.1 %reshape.19 = bf16[32,32,2,64]{3,2,1,0:T(2,128)(2,1)} reshape(bf16[1024,128]{1,0:T(8,128)(2,1)S(1)} %shard_map.110) | data formatting | bytes 524288 | tf_op jit(solution)/shard_map/reshape | solution.py:437
Async XLA Ops:
  0.0 2.8 %copy-start.5 = (bf16[1,1,1024,128]{3,2,1,0:T(8,128)(2,1)S(1)}, bf16[1,1,1024,128]{3,2,1,0:T(8,128)(2,1)}, u32[]{:S(2)}) copy-start(bf16[1,1,1024,128]{3,2,1,0:T(8,128)(2,1)} %param.11) | copy-start | bytes 786436
  2.7 0.7 %copy-start.7 = (s32[1,1,8,256]{3,2,1,0:T(8,128)S(1)}, s32[1,1,8,256]{3,2,1,0:T(8,128)}, u32[]{:S(2)}) copy-start(s32[1,1,8,256]{3,2,1,0:T(8,128)} %param.12) | copy-start | bytes 24580
  3.4 21.4 %copy-start = (bf16[3,3,256,128]{3,2,1,0:T(8,128)(2,1)S(1)}, bf16[3,3,256,128]{3,2,1,0:T(8,128)(2,1)}, u32[]{:S(2)}) copy-start(bf16[3,3,256,128]{3,2,1,0:T(8,128)(2,1)} %w_d1.1) | copy-start | bytes 1769476
  3.4 21.4 %copy-start.1 = (bf16[3,3,128,128]{3,2,1,0:T(8,128)(2,1)S(1)}, bf16[3,3,128,128]{3,2,1,0:T(8,128)(2,1)}, u32[]{:S(2)}) copy-start(bf16[3,3,128,128]{3,2,1,0:T(8,128)(2,1)} %w_enc.1) | copy-start | bytes 884740
  3.4 21.4 %copy-start.2 = (bf16[3,3,128,128]{3,2,1,0:T(8,128)(2,1)S(1)}, bf16[3,3,128,128]{3,2,1,0:T(8,128)(2,1)}, u32[]{:S(2)}) copy-start(bf16[3,3,128,128]{3,2,1,0:T(8,128)(2,1)} %w_m1.1) | copy-start | bytes 884740
  3.4 21.4 %copy-start.3 = (bf16[3,3,128,128]{3,2,1,0:T(8,128)(2,1)S(1)}, bf16[3,3,128,128]{3,2,1,0:T(8,128)(2,1)}, u32[]{:S(2)}) copy-start(bf16[3,3,128,128]{3,2,1,0:T(8,128)(2,1)} %w_m2.1) | copy-start | bytes 884740
  3.4 21.4 %copy-start.4 = (bf16[3,3,128,128]{3,2,1,0:T(8,128)(2,1)S(1)}, bf16[3,3,128,128]{3,2,1,0:T(8,128)(2,1)}, u32[]{:S(2)}) copy-start(bf16[3,3,128,128]{3,2,1,0:T(8,128)(2,1)} %w_d2.1) | copy-start | bytes 884740
  3.4 21.4 %copy-start.6 = (bf16[3,3,64,128]{3,2,1,0:T(8,128)(2,1)S(1)}, bf16[3,3,64,128]{3,2,1,0:T(8,128)(2,1)}, u32[]{:S(2)}) copy-start(bf16[3,3,64,128]{3,2,1,0:T(8,128)(2,1)} %w_in.1) | copy-start | bytes 442372

commit v3 on v2

--- a/solution.py
+++ b/solution.py
@@ -18,7 +18,7 @@
 
 def unet_kernel(
     tile_rows, tile_cols, p_ref, w_in, w_enc, w_m1, w_m2, w_d1, w_d2, w_out, out_ref,
-    first, skip, pooled, middle, up, dec1, tmp, c_in, c_enc, c_m1, c_m2, c_d1u, c_d1s, c_d2, c_out,
+    first, skip, pooled, middle, up, dec1, tmp, c_in, c_enc, c_m1, c_m2, c_d1, c_d2, c_out, pairs,
 ):
     wide = tile_cols + 2 * HALO
     half = wide // 2
@@ -29,33 +29,37 @@
 
     c_in[...] = jnp.zeros_like(c_in)
     c_out[...] = jnp.zeros_like(c_out)
+    w_last = w_out[...].astype(f32).T.astype(bf16)
     for b in range(2):
-        c_out[b * CH : (b + 1) * CH, b * FIELDS : (b + 1) * FIELDS] = w_out[...]
+        c_out[b * CH : (b + 1) * CH, b * FIELDS : (b + 1) * FIELDS] = w_last
+    size = p_ref.shape[0]
+    values = p_ref[...].astype(f32)
+    turned = pltpu.roll(values, FIELDS, 1)
+    below = pltpu.roll(values, size - wide, 0)
+    turned_below = pltpu.roll(turned, size - wide, 0)
+    low = lax.broadcasted_iota(jnp.int32, (size, CH), 1) < FIELDS
+    pairs[0] = jnp.where(low, values, turned_below).astype(bf16)
+    pairs[1] = jnp.where(low, turned, below).astype(bf16)
     for dy in range(3):
         for dx in range(3):
             rows = slice(dy * CH, (dy + 1) * CH)
             cols = slice(dx * CH, (dx + 1) * CH)
-            for b in range(2):
-                c_in[b, dy * CH + b * FIELDS : dy * CH + (b + 1) * FIELDS, cols] = w_in[dy, dx]
+            c_in[dy * FIELDS : (dy + 1) * FIELDS, cols] = w_in[dy, dx]
             c_enc[rows, cols] = w_enc[dy, dx]
             c_m1[rows, cols] = w_m1[dy, dx]
             c_m2[rows, cols] = w_m2[dy, dx]
-            c_d1u[rows, cols] = w_d1[dy, dx, :CH]
-            c_d1s[rows, cols] = w_d1[dy, dx, CH:]
+            c_d1[rows, cols] = w_d1[dy, dx, :CH]
+            c_d1[(dy + 3) * CH : (dy + 4) * CH, cols] = w_d1[dy, dx, CH:]
             c_d2[rows, cols] = w_d2[dy, dx]
 
-    def conv(sources, width, chunk_rows, start):
+    def conv(sources, weight, width, chunk_rows, start, steps=(0, 1, 2)):
         size = chunk_rows * width
-        u = None
-        for load, weight, offset in sources:
-            windows = [
-                load(pl.multiple_of(start + (offset + dy) * width, 8), size).astype(bf16)
-                for dy in range(3)
-            ]
-            part = jnp.dot(
-                jnp.concatenate(windows, axis=1), weight[...], preferred_element_type=f32
-            )
-            u = part if u is None else u + part
+        windows = [
+            load(pl.multiple_of(start + (offset + dy) * width, 8), size).astype(bf16)
+            for load, offset in sources
+            for dy in steps
+        ]
+        u = jnp.dot(jnp.concatenate(windows, axis=1), weight[...], preferred_element_type=f32)
         return silu(
             u[:, CH : 2 * CH]
             + pltpu.roll(u[:, :CH], 1, 0)
@@ -92,9 +96,7 @@
 
     def first_step(b, start):
         chunk = h_first // 2
-        value = conv(
-            [(lambda s, n: p_ref[pl.ds(s, n), :], c_in.at[b], 0)], wide, chunk, start
-        )
+        value = conv([(reader(pairs, b), 0)], c_in, wide, chunk, start, (0, 2))
         first[b, pl.ds(start, chunk * wide), :] = value.astype(bf16)
 
     per_chunk(h_first, h_first // 2, wide, first_step)
@@ -102,7 +104,7 @@
 
     def skip_step(b, start):
         chunk = h_skip // 2
-        value = conv([(reader(first, b), c_enc, 0)], wide, chunk, start)
+        value = conv([(reader(first, b), 0)], c_enc, wide, chunk, start)
         skip[b, pl.ds(start, chunk * wide), :] = value.astype(bf16)
 
     per_chunk(h_skip, h_skip // 2, wide, skip_step)
@@ -118,7 +120,7 @@
         pooled[b] = (total * 0.25).astype(bf16).astype(f32)
 
     def mid_step(b, start):
-        value = conv([(reader(pooled, b), c_m1, 0)], half, h_mid, start)
+        value = conv([(reader(pooled, b), 0)], c_m1, half, h_mid, start)
         middle[b, pl.ds(start, h_mid * half), :] = value.astype(bf16).astype(f32)
 
     per_chunk(h_mid, h_mid, half, mid_step)
@@ -126,7 +128,7 @@
 
     @pl.loop(0, 2)
     def _(b):
-        value = conv([(reader(middle, b), c_m2, 0)], half, h_coarse, 0)
+        value = conv([(reader(middle, b), 0)], c_m2, half, h_coarse, 0)
         size = h_coarse * half
         tmp[pl.ds(0, size, stride=2), :] = value
         tmp[pl.ds(1, size, stride=2), :] = value
@@ -137,9 +139,7 @@
 
     def dec1_step(b, start):
         chunk = h_dec1 // 2
-        value = conv(
-            [(reader(up, b), c_d1u, 0), (reader(skip, b), c_d1s, 4)], wide, chunk, start
-        )
+        value = conv([(reader(up, b), 0), (reader(skip, b), 4)], c_d1, wide, chunk, start)
         dec1[b, pl.ds(start, chunk * wide), :] = value.astype(bf16)
 
     per_chunk(h_dec1, h_dec1 // 2, wide, dec1_step)
@@ -152,7 +152,7 @@
         start = pl.multiple_of(i * (chunk * wide), 8)
         both = []
         for b in range(2):
-            value = conv([(reader(dec1, b), c_d2, 0)], wide, chunk, start)
+            value = conv([(reader(dec1, b), 0)], c_d2, wide, chunk, start)
             value = value.reshape(chunk, wide, CH)[:, HALO : HALO + tile_cols]
             both.append(value.reshape(chunk * tile_cols, CH).astype(bf16))
         result = jnp.dot(
@@ -175,9 +175,12 @@
         pltpu.VMEM((2, (tile_rows + 4) * wide, CH), bf16),
         pltpu.VMEM((2, (tile_rows + 2) * wide, CH), bf16),
         pltpu.VMEM(((tile_rows // 2 + 6) * wide, CH), f32),
-        pltpu.VMEM((2, 3 * CH, 3 * CH), bf16),
-        square, square, square, square, square, square,
+        pltpu.VMEM((4 * FIELDS, 3 * CH), bf16),
+        square, square, square,
+        pltpu.VMEM((6 * CH, 3 * CH), bf16),
+        square,
         pltpu.VMEM((2 * CH, 2 * FIELDS), bf16),
+        pltpu.VMEM((2, (tile_rows + 2 * HALO) * wide, CH), bf16),
     ]
     return pl.pallas_call(
         functools.partial(unet_kernel, tile_rows, tile_cols),
@@ -189,7 +192,7 @@
         cost_estimate=pl.CostEstimate(
             flops=6 * 10**9, bytes_accessed=4 * 10**6, transcendentals=2 * 10**6
         ),
-    )(padded, *weights)
+    )(padded, *weights[:-1], weights[-1].T)
 
 
 MESH = pl.DeviceIdType.MESH
@@ -197,7 +200,7 @@
 
 def regrid_kernel(
     tile_rows, tile_cols, src_ref, req_ref, sten_ref, wgt_ref, out_ref,
-    reqs, src_t, mix, outbox, inbox, acc, pad,
+    reqs, src_t, mix, outbox, inbox, acc, pad, slot_rows, weight_rows,
     req_send, req_recv, box_send, box_recv, halo_send, halo_recv,
 ):
     f32, bf16 = jnp.float32, jnp.bfloat16
@@ -252,22 +255,44 @@
     reqs[me] = req_ref[...]
     src_t[...] = src_ref[...].astype(f32).T.astype(bf16)
 
+    taps = sten_ref.shape[1]
+    for k in range(taps):
+        slot_rows[k : k + 1, :] = jnp.concatenate(
+            [sten_ref[y, k : k + 1, :] for y in range(tile_rows)], axis=1
+        ).astype(f32)
+        weight_rows[k : k + 1, :] = jnp.concatenate(
+            [wgt_ref[y, k : k + 1, :] for y in range(tile_rows)], axis=1
+        )
+    piece = 256
+
+    def hits(values, base, width):
+        ids = lax.broadcasted_iota(jnp.int32, (piece, width), 0).astype(f32).astype(bf16)
+        near = jnp.broadcast_to(values - jnp.asarray(base, jnp.int32).astype(f32), (piece, width))
+        return ids == near.astype(bf16)
+
     def mix_block(j):
-        slots = lax.broadcasted_iota(jnp.int32, (cap, spots), 0)
-        total = None
-        for k in range(sten_ref.shape[0]):
-            hit = slots == sten_ref[k : k + 1, :] - j * cap
-            part = jnp.where(hit, wgt_ref[k : k + 1, :], 0.0)
-            total = part if total is None else total + part
-        mix[j] = total.astype(bf16)
+        for start in range(0, cap, piece):
+            total = None
+            for k in range(taps):
+                hit = hits(slot_rows[k : k + 1, :], j * cap + start, spots)
+                weight = jnp.broadcast_to(weight_rows[k : k + 1, :], (piece, spots)).astype(bf16)
+                part = jnp.where(hit, weight, jnp.zeros((), bf16))
+                total = part if total is None else total + part
+            mix[j, start : start + piece] = total
 
     @pl.loop(0, n // 2)
     def _(j):
         mix_block(j)
 
     def picked(dest):
-        ids = lax.broadcasted_iota(jnp.int32, (cells, cap), 0)
-        hot = jnp.where(ids == reqs[dest, pl.ds(me, 1), :], 1.0, 0.0).astype(bf16)
+        asked = reqs[dest, pl.ds(me, 1), :].astype(f32)
+        hot = jnp.concatenate(
+            [
+                jnp.where(hits(asked, start, cap), jnp.ones((), bf16), jnp.zeros((), bf16))
+                for start in range(0, cells, piece)
+            ],
+            axis=0,
+        )
         return jnp.dot(src_t[...], hot, preferred_element_type=f32).astype(bf16)
 
     def post(step, sender):
@@ -411,6 +436,8 @@
             pltpu.VMEM((n, columns, cap), bf16),
             pltpu.VMEM((columns, spots), f32),
             pltpu.VMEM((blocks + 2, rows * HALO, columns), bf16),
+            pltpu.VMEM((stencil.shape[1], spots), f32),
+            pltpu.VMEM((stencil.shape[1], spots), f32),
             dma((n,)), dma((n,)), dma((n,)), dma((n,)), dma((8,)), dma((8,)),
         ],
         compiler_params=pltpu.CompilerParams(
@@ -423,13 +450,13 @@
 
 
 def body(source_tiles, requests, stencil, regrid_weight, *weights):
-    tile_rows, tile_cols, taps = stencil.shape
+    tile_rows, tile_cols = stencil.shape[:2]
     cells, columns = source_tiles.shape[2:]
     padded = regrid(
         source_tiles.reshape(cells, columns),
         requests.reshape(requests.shape[2:]),
-        stencil.transpose(2, 0, 1).reshape(taps, -1),
-        regrid_weight.transpose(2, 0, 1).reshape(taps, -1),
+        stencil.transpose(0, 2, 1),
+        regrid_weight.transpose(0, 2, 1),
         tile_rows,
         tile_cols,
     )

time: 41 us -> 39.1 us (0.954)
  Pallas kernels: 36.2 us -> 34.3 us
    pallas_call x1, Pallas kernels: 14.8 us -> 13 us  [unet(): pl.pallas_call(functools.partial(unet_kernel, tile_rows, tile_cols), out_...]
    unnamed x17 -> x22, local copies, waits for them, and re-layouts: 1.49 us -> 3.35 us
    transpose x2 -> x0, local copies, waits for them, and re-layouts: 1.7 us -> none  [the longest x1 0.86 us: body(): stencil.transpose(2, 0, 1).reshape(taps, -1)]
where the time goes in v3:
time: 39.1 us; the launch traced here: 38.8 us
  Pallas kernels  34.3 us (88%)
  local copies, waits for them, and re-layouts  4.41 us (11%)
    pallas_call x1, Pallas kernels, regrid(): pl.pallas_call(functools.partial(regrid_kernel, tile_rows, tile_cols), ou...  21.3 us
    pallas_call x1, Pallas kernels, unet(): pl.pallas_call(functools.partial(unet_kernel, tile_rows, tile_cols), out_...  13 us
    unnamed x22, local copies, waits for them, and re-layouts  3.35 us
    reshape x1, local copies, waits for them, and re-layouts, body(): return result.reshape(tile_rows, tile_cols, 2, FIELDS)  1.06 us

profile of v3, /device:TPU:0, one launch (start us, length us, event | category | flops | bytes accessed | tf_op | source)
XLA Modules:
  0.0 38.8 jit_solution(7099471731333869345)
XLA Ops:
  0.0 0.0 copy-start.10
  0.0 0.7 %copy-done.10 = s32[1,1,8,256]{3,2,1,0:T(8,128)S(1)} copy-done((s32[1,1,8,256]{3,2,1,0:T(8,128)S(1)}, s32[1,1,8,256]{3,2,1,0:T(8,128)}, u32[]{:S(2)}) %copy-start.10) | copy-done | bytes 8216
  0.7 0.0 copy-start.5
  0.7 0.9 %copy-done.5 = bf16[1,1,1024,128]{3,2,1,0:T(8,128)(2,1)S(1)} copy-done((bf16[1,1,1024,128]{3,2,1,0:T(8,128)(2,1)S(1)}, bf16[1,1,1024,128]{3,2,1,0:T(8,128)(2,1)}, u32[]{:S(2)}) %copy-start.5) | copy-done | bytes 262168
  1.6 0.0 copy-start.7
  1.7 0.8 %copy-done.7 = s32[32,32,4]{1,2,0:T(4,128)S(1)} copy-done((s32[32,32,4]{1,2,0:T(4,128)S(1)}, s32[32,32,4]{1,2,0:T(4,128)}, u32[]{:S(2)}) %copy-start.7) | copy-done | bytes 16408
  2.5 0.0 copy-start.8
  2.5 0.8 %copy-done.8 = f32[32,32,4]{1,2,0:T(4,128)S(1)} copy-done((f32[32,32,4]{1,2,0:T(4,128)S(1)}, f32[32,32,4]{1,2,0:T(4,128)}, u32[]{:S(2)}) %copy-start.8) | copy-done | bytes 16408
  3.3 0.0 copy-start
  3.3 0.0 copy-start.1
  3.3 0.0 copy-start.2
  3.3 0.0 copy-start.3
  3.3 0.0 copy-start.4
  3.3 0.0 copy-start.6
  3.4 0.0 copy-start.9
  3.4 21.3 %shard_map.109.p_ref = bf16[2304,128]{1,0:T(8,128)(2,1)S(1)} custom-call(bf16[1024,128]{1,0:T(8,128)(2,1)S(1)} %bitcast.5, s32[8,256]{1,0:T(8,128)S(1)} %bitcast.9, s32[32,4,32]{2,1,0:T(4,128)S(1)} %bitcast.6, f32[32,4,32]{2,1,0:T(4,128)S(1)} %bitcast.7), custom_call_target="tpu_custom_call" | custom-call | flops 1000000000 | bytes 2000000 | tf_op jit(solution)/shard_map/pallas_call | solution.py:426
  24.7 0.0 copy-done
  24.7 0.0 copy-done.1
  24.7 0.0 copy-done.2
  24.7 0.0 copy-done.3
  24.7 0.0 copy-done.4
  24.7 0.0 copy-done.6
  24.8 0.0 copy-done.9
  24.8 13.0 %shard_map.110 = bf16[1024,128]{1,0:T(8,128)(2,1)S(1)} custom-call(bf16[2304,128]{1,0:T(8,128)(2,1)S(1)} %shard_map.109.p_ref, bf16[3,3,64,128]{3,2,1,0:T(8,128)(2,1)S(1)} %copy-done.6, bf16[3,3,128,128]{3,2,1,0:T(8,128)(2,1)S(1)} %copy-done.1, bf16[3,3,128,128]{3,2,1,0:T(8,128)(2,1)S(1)} %copy-done.2, bf16[3,3,128,128]{3,2,1,0:T(8,128)(2,1)S(1)} %copy-done.3, ...), custom_call_target="tpu_custom_call" | custom-call | flops 6000000000 | bytes 4000000 | tf_op jit(solution)/shard_map/pallas_call | solution.py:185
  37.7 1.1 %reshape.11 = bf16[32,32,2,64]{3,2,1,0:T(2,128)(2,1)} reshape(bf16[1024,128]{1,0:T(8,128)(2,1)S(1)} %shard_map.110) | data formatting | bytes 524288 | tf_op jit(solution)/shard_map/reshape | solution.py:464
Async XLA Ops:
  0.0 0.7 %copy-start.10 = (s32[1,1,8,256]{3,2,1,0:T(8,128)S(1)}, s32[1,1,8,256]{3,2,1,0:T(8,128)}, u32[]{:S(2)}) copy-start(s32[1,1,8,256]{3,2,1,0:T(8,128)} %param.12) | copy-start | bytes 24580
  0.7 0.9 %copy-start.5 = (bf16[1,1,1024,128]{3,2,1,0:T(8,128)(2,1)S(1)}, bf16[1,1,1024,128]{3,2,1,0:T(8,128)(2,1)}, u32[]{:S(2)}) copy-start(bf16[1,1,1024,128]{3,2,1,0:T(8,128)(2,1)} %param.11) | copy-start | bytes 786436
  1.6 0.8 %copy-start.7 = (s32[32,32,4]{1,2,0:T(4,128)S(1)}, s32[32,32,4]{1,2,0:T(4,128)}, u32[]{:S(2)}) copy-start(s32[32,32,4]{1,2,0:T(4,128)} %param.13) | copy-start | bytes 49156
  2.5 0.8 %copy-start.8 = (f32[32,32,4]{1,2,0:T(4,128)S(1)}, f32[32,32,4]{1,2,0:T(4,128)}, u32[]{:S(2)}) copy-start(f32[32,32,4]{1,2,0:T(4,128)} %param.14) | copy-start | bytes 49156
  3.3 21.4 %copy-start = (bf16[3,3,256,128]{3,2,1,0:T(8,128)(2,1)S(1)}, bf16[3,3,256,128]{3,2,1,0:T(8,128)(2,1)}, u32[]{:S(2)}) copy-start(bf16[3,3,256,128]{3,2,1,0:T(8,128)(2,1)} %w_d1.1) | copy-start | bytes 1769476
  3.3 21.4 %copy-start.1 = (bf16[3,3,128,128]{3,2,1,0:T(8,128)(2,1)S(1)}, bf16[3,3,128,128]{3,2,1,0:T(8,128)(2,1)}, u32[]{:S(2)}) copy-start(bf16[3,3,128,128]{3,2,1,0:T(8,128)(2,1)} %w_enc.1) | copy-start | bytes 884740
  3.3 21.4 %copy-start.2 = (bf16[3,3,128,128]{3,2,1,0:T(8,128)(2,1)S(1)}, bf16[3,3,128,128]{3,2,1,0:T(8,128)(2,1)}, u32[]{:S(2)}) copy-start(bf16[3,3,128,128]{3,2,1,0:T(8,128)(2,1)} %w_m1.1) | copy-start | bytes 884740
  3.3 21.4 %copy-start.3 = (bf16[3,3,128,128]{3,2,1,0:T(8,128)(2,1)S(1)}, bf16[3,3,128,128]{3,2,1,0:T(8,128)(2,1)}, u32[]{:S(2)}) copy-start(bf16[3,3,128,128]{3,2,1,0:T(8,128)(2,1)} %w_m2.1) | copy-start | bytes 884740
  3.3 21.4 %copy-start.4 = (bf16[3,3,128,128]{3,2,1,0:T(8,128)(2,1)S(1)}, bf16[3,3,128,128]{3,2,1,0:T(8,128)(2,1)}, u32[]{:S(2)}) copy-start(bf16[3,3,128,128]{3,2,1,0:T(8,128)(2,1)} %w_d2.1) | copy-start | bytes 884740
  3.3 21.4 %copy-start.6 = (bf16[3,3,64,128]{3,2,1,0:T(8,128)(2,1)S(1)}, bf16[3,3,64,128]{3,2,1,0:T(8,128)(2,1)}, u32[]{:S(2)}) copy-start(bf16[3,3,64,128]{3,2,1,0:T(8,128)(2,1)} %w_in.1) | copy-start | bytes 442372
  3.4 21.4 %copy-start.9 = (bf16[128,64]{0,1:T(8,128)(2,1)S(1)}, bf16[128,64]{0,1:T(8,128)(2,1)}, u32[]{:S(2)}) copy-start(bf16[128,64]{0,1:T(8,128)(2,1)} %param.21) | copy-start | bytes 49156

commit v4 on v3

--- a/solution.py
+++ b/solution.py
@@ -199,8 +199,8 @@
 
 
 def regrid_kernel(
-    tile_rows, tile_cols, src_ref, req_ref, sten_ref, wgt_ref, out_ref,
-    reqs, src_t, mix, outbox, inbox, acc, pad, slot_rows, weight_rows,
+    tile_rows, tile_cols, src_in, req_in, sten_in, wgt_in, out_ref,
+    src_ref, req_ref, sten_ref, wgt_ref, load, reqs, src_t, mix, outbox, inbox, acc, pad, slot_rows, weight_rows,
     req_send, req_recv, box_send, box_recv, halo_send, halo_recv,
 ):
     f32, bf16 = jnp.float32, jnp.bfloat16
@@ -214,6 +214,15 @@
     edge = HALO * HALO
     inner = tile_rows * HALO
 
+    loads = [
+        pltpu.make_async_copy(outer, held, load.at[i])
+        for i, (outer, held) in enumerate(
+            [(req_in, req_ref), (src_in, src_ref), (sten_in, sten_ref), (wgt_in, wgt_ref)]
+        )
+    ]
+    for copy in loads:
+        copy.start()
+
     barrier = pltpu.get_barrier_semaphore()
 
     def greet(r, c):
@@ -237,6 +246,8 @@
 
     rows_beside = jnp.minimum(row, 1) + jnp.minimum(n_row - 1 - row, 1)
     pl.semaphore_wait(barrier, n - 1 + 3 * rows_beside)
+
+    loads[0].wait()
 
     def ask(step, sender):
         return pltpu.make_async_remote_copy(
@@ -253,8 +264,11 @@
         ask(step, me).start()
 
     reqs[me] = req_ref[...]
+    loads[1].wait()
     src_t[...] = src_ref[...].astype(f32).T.astype(bf16)
 
+    loads[2].wait()
+    loads[3].wait()
     taps = sten_ref.shape[1]
     for k in range(taps):
         slot_rows[k : k + 1, :] = jnp.concatenate(
@@ -263,22 +277,32 @@
         weight_rows[k : k + 1, :] = jnp.concatenate(
             [wgt_ref[y, k : k + 1, :] for y in range(tile_rows)], axis=1
         )
-    piece = 256
-
-    def hits(values, base, width):
-        ids = lax.broadcasted_iota(jnp.int32, (piece, width), 0).astype(f32).astype(bf16)
-        near = jnp.broadcast_to(values - jnp.asarray(base, jnp.int32).astype(f32), (piece, width))
-        return ids == near.astype(bf16)
+    tile, piece = 16, 256
+
+    def ladder(width):
+        return lax.broadcasted_iota(jnp.int32, (tile, width), 0).astype(f32).astype(bf16)
+
+    def spread(values):
+        return jnp.broadcast_to(values, (tile, values.shape[1])).astype(bf16)
+
+    lanes = min(512, spots)
+    zero, one = jnp.zeros((), bf16), jnp.ones((), bf16)
 
     def mix_block(j):
-        for start in range(0, cap, piece):
-            total = None
-            for k in range(taps):
-                hit = hits(slot_rows[k : k + 1, :], j * cap + start, spots)
-                weight = jnp.broadcast_to(weight_rows[k : k + 1, :], (piece, spots)).astype(bf16)
-                part = jnp.where(hit, weight, jnp.zeros((), bf16))
-                total = part if total is None else total + part
-            mix[j, start : start + piece] = total
+        for left_lane in range(0, spots, lanes):
+            here = slice(left_lane, left_lane + lanes)
+            ids = ladder(lanes)
+            weights = [spread(weight_rows[k : k + 1, here]) for k in range(taps)]
+            for start in range(0, cap, piece):
+                base = (j * cap + start).astype(f32)
+                near = [spread(slot_rows[k : k + 1, here] - base) for k in range(taps)]
+                for g in range(0, min(piece, cap), tile):
+                    step_ids = ids + jnp.asarray(g, bf16)
+                    total = None
+                    for k in range(taps):
+                        part = jnp.where(step_ids == near[k], weights[k], zero)
+                        total = part if total is None else total + part
+                    mix[j, start + g : start + g + tile, here] = total
 
     @pl.loop(0, n // 2)
     def _(j):
@@ -286,13 +310,13 @@
 
     def picked(dest):
         asked = reqs[dest, pl.ds(me, 1), :].astype(f32)
-        hot = jnp.concatenate(
-            [
-                jnp.where(hits(asked, start, cap), jnp.ones((), bf16), jnp.zeros((), bf16))
-                for start in range(0, cells, piece)
-            ],
-            axis=0,
-        )
+        ids = ladder(cap)
+        rows = []
+        for start in range(0, cells, piece):
+            near = spread(asked - float(start))
+            for g in range(0, piece, tile):
+                rows.append(jnp.where(ids + jnp.asarray(g, bf16) == near, one, zero))
+        hot = jnp.concatenate(rows, axis=0)
         return jnp.dot(src_t[...], hot, preferred_element_type=f32).astype(bf16)
 
     def post(step, sender):
@@ -426,9 +450,14 @@
     return pl.pallas_call(
         functools.partial(regrid_kernel, tile_rows, tile_cols),
         out_shape=jax.ShapeDtypeStruct((rows * (tile_cols + 2 * HALO), columns), bf16),
-        in_specs=[pl.BlockSpec(memory_space=pltpu.VMEM)] * 4,
+        in_specs=[pl.BlockSpec(memory_space=pltpu.HBM)] * 4,
         out_specs=pl.BlockSpec(memory_space=pltpu.VMEM),
         scratch_shapes=[
+            pltpu.VMEM(source.shape, bf16),
+            pltpu.VMEM(wanted.shape, jnp.int32),
+            pltpu.VMEM(stencil.shape, jnp.int32),
+            pltpu.VMEM(weight.shape, f32),
+            dma((4,)),
             pltpu.VMEM((n, n, cap), jnp.int32),
             pltpu.VMEM((columns, cells), bf16),
             pltpu.VMEM((n, cap, spots), bf16),

time: 39.1 us -> 39.3 us (level)
  no operation moved by 1% of the time
where the time goes in v4:
time: 39.3 us; the launch traced here: 39 us
  Pallas kernels  34.5 us (88%)
  local copies, waits for them, and re-layouts  4.41 us (11%)
    pallas_call x1, Pallas kernels, regrid(): pl.pallas_call(functools.partial(regrid_kernel, tile_rows, tile_cols), ou...  21.6 us
    pallas_call x1, Pallas kernels, unet(): pl.pallas_call(functools.partial(unet_kernel, tile_rows, tile_cols), out_...  13 us
    unnamed x22, local copies, waits for them, and re-layouts  3.35 us
    reshape x1, local copies, waits for them, and re-layouts, body(): return result.reshape(tile_rows, tile_cols, 2, FIELDS)  1.06 us

profile of v4, /device:TPU:0, one launch (start us, length us, event | category | flops | bytes accessed | tf_op | source)
XLA Modules:
  0.0 39.0 jit_solution(10883566661578523295)
XLA Ops:
  0.0 0.0 copy-start.10
  0.0 0.7 %copy-done.10 = s32[1,1,8,256]{3,2,1,0:T(8,128)S(1)} copy-done((s32[1,1,8,256]{3,2,1,0:T(8,128)S(1)}, s32[1,1,8,256]{3,2,1,0:T(8,128)}, u32[]{:S(2)}) %copy-start.10) | copy-done | bytes 8216
  0.7 0.0 copy-start.5
  0.7 0.9 %copy-done.5 = bf16[1,1,1024,128]{3,2,1,0:T(8,128)(2,1)S(1)} copy-done((bf16[1,1,1024,128]{3,2,1,0:T(8,128)(2,1)S(1)}, bf16[1,1,1024,128]{3,2,1,0:T(8,128)(2,1)}, u32[]{:S(2)}) %copy-start.5) | copy-done | bytes 262168
  1.6 0.0 copy-start.7
  1.7 0.8 %copy-done.7 = s32[32,32,4]{1,2,0:T(4,128)S(1)} copy-done((s32[32,32,4]{1,2,0:T(4,128)S(1)}, s32[32,32,4]{1,2,0:T(4,128)}, u32[]{:S(2)}) %copy-start.7) | copy-done | bytes 16408
  2.5 0.0 copy-start.8
  2.5 0.8 %copy-done.8 = f32[32,32,4]{1,2,0:T(4,128)S(1)} copy-done((f32[32,32,4]{1,2,0:T(4,128)S(1)}, f32[32,32,4]{1,2,0:T(4,128)}, u32[]{:S(2)}) %copy-start.8) | copy-done | bytes 16408
  3.3 0.0 copy-start
  3.3 0.0 copy-start.1
  3.3 0.0 copy-start.2
  3.3 0.0 copy-start.3
  3.3 0.0 copy-start.4
  3.3 0.0 copy-start.6
  3.4 0.0 copy-start.9
  3.4 21.6 %shard_map.109.p_ref = bf16[2304,128]{1,0:T(8,128)(2,1)S(1)} custom-call(bf16[1024,128]{1,0:T(8,128)(2,1)S(1)} %bitcast.5, s32[8,256]{1,0:T(8,128)S(1)} %bitcast.9, s32[32,4,32]{2,1,0:T(4,128)S(1)} %bitcast.6, f32[32,4,32]{2,1,0:T(4,128)S(1)} %bitcast.7), custom_call_target="tpu_custom_call" | custom-call | flops 1000000000 | bytes 2000000 | tf_op jit(solution)/shard_map/pallas_call | solution.py:450
  24.9 0.0 copy-done
  25.0 0.0 copy-done.1
  25.0 0.0 copy-done.2
  25.0 0.0 copy-done.3
  25.0 0.0 copy-done.4
  25.0 0.0 copy-done.6
  25.0 0.0 copy-done.9
  25.0 13.0 %shard_map.110 = bf16[1024,128]{1,0:T(8,128)(2,1)S(1)} custom-call(bf16[2304,128]{1,0:T(8,128)(2,1)S(1)} %shard_map.109.p_ref, bf16[3,3,64,128]{3,2,1,0:T(8,128)(2,1)S(1)} %copy-done.6, bf16[3,3,128,128]{3,2,1,0:T(8,128)(2,1)S(1)} %copy-done.1, bf16[3,3,128,128]{3,2,1,0:T(8,128)(2,1)S(1)} %copy-done.2, bf16[3,3,128,128]{3,2,1,0:T(8,128)(2,1)S(1)} %copy-done.3, ...), custom_call_target="tpu_custom_call" | custom-call | flops 6000000000 | bytes 4000000 | tf_op jit(solution)/shard_map/pallas_call | solution.py:185
  38.0 1.1 %reshape.11 = bf16[32,32,2,64]{3,2,1,0:T(2,128)(2,1)} reshape(bf16[1024,128]{1,0:T(8,128)(2,1)S(1)} %shard_map.110) | data formatting | bytes 524288 | tf_op jit(solution)/shard_map/reshape | solution.py:493
Async XLA Ops:
  0.0 0.7 %copy-start.10 = (s32[1,1,8,256]{3,2,1,0:T(8,128)S(1)}, s32[1,1,8,256]{3,2,1,0:T(8,128)}, u32[]{:S(2)}) copy-start(s32[1,1,8,256]{3,2,1,0:T(8,128)} %param.12) | copy-start | bytes 24580
  0.7 0.9 %copy-start.5 = (bf16[1,1,1024,128]{3,2,1,0:T(8,128)(2,1)S(1)}, bf16[1,1,1024,128]{3,2,1,0:T(8,128)(2,1)}, u32[]{:S(2)}) copy-start(bf16[1,1,1024,128]{3,2,1,0:T(8,128)(2,1)} %param.11) | copy-start | bytes 786436
  1.6 0.8 %copy-start.7 = (s32[32,32,4]{1,2,0:T(4,128)S(1)}, s32[32,32,4]{1,2,0:T(4,128)}, u32[]{:S(2)}) copy-start(s32[32,32,4]{1,2,0:T(4,128)} %param.13) | copy-start | bytes 49156
  2.5 0.8 %copy-start.8 = (f32[32,32,4]{1,2,0:T(4,128)S(1)}, f32[32,32,4]{1,2,0:T(4,128)}, u32[]{:S(2)}) copy-start(f32[32,32,4]{1,2,0:T(4,128)} %param.14) | copy-start | bytes 49156
  3.3 21.6 %copy-start = (bf16[3,3,256,128]{3,2,1,0:T(8,128)(2,1)S(1)}, bf16[3,3,256,128]{3,2,1,0:T(8,128)(2,1)}, u32[]{:S(2)}) copy-start(bf16[3,3,256,128]{3,2,1,0:T(8,128)(2,1)} %w_d1.1) | copy-start | bytes 1769476
  3.3 21.6 %copy-start.1 = (bf16[3,3,128,128]{3,2,1,0:T(8,128)(2,1)S(1)}, bf16[3,3,128,128]{3,2,1,0:T(8,128)(2,1)}, u32[]{:S(2)}) copy-start(bf16[3,3,128,128]{3,2,1,0:T(8,128)(2,1)} %w_enc.1) | copy-start | bytes 884740
  3.3 21.6 %copy-start.2 = (bf16[3,3,128,128]{3,2,1,0:T(8,128)(2,1)S(1)}, bf16[3,3,128,128]{3,2,1,0:T(8,128)(2,1)}, u32[]{:S(2)}) copy-start(bf16[3,3,128,128]{3,2,1,0:T(8,128)(2,1)} %w_m1.1) | copy-start | bytes 884740
  3.3 21.6 %copy-start.3 = (bf16[3,3,128,128]{3,2,1,0:T(8,128)(2,1)S(1)}, bf16[3,3,128,128]{3,2,1,0:T(8,128)(2,1)}, u32[]{:S(2)}) copy-start(bf16[3,3,128,128]{3,2,1,0:T(8,128)(2,1)} %w_m2.1) | copy-start | bytes 884740
  3.3 21.6 %copy-start.4 = (bf16[3,3,128,128]{3,2,1,0:T(8,128)(2,1)S(1)}, bf16[3,3,128,128]{3,2,1,0:T(8,128)(2,1)}, u32[]{:S(2)}) copy-start(bf16[3,3,128,128]{3,2,1,0:T(8,128)(2,1)} %w_d2.1) | copy-start | bytes 884740
  3.3 21.6 %copy-start.6 = (bf16[3,3,64,128]{3,2,1,0:T(8,128)(2,1)S(1)}, bf16[3,3,64,128]{3,2,1,0:T(8,128)(2,1)}, u32[]{:S(2)}) copy-start(bf16[3,3,64,128]{3,2,1,0:T(8,128)(2,1)} %w_in.1) | copy-start | bytes 442372
  3.4 21.6 %copy-start.9 = (bf16[128,64]{0,1:T(8,128)(2,1)S(1)}, bf16[128,64]{0,1:T(8,128)(2,1)}, u32[]{:S(2)}) copy-start(bf16[128,64]{0,1:T(8,128)(2,1)} %param.21) | copy-start | bytes 49156

commit v5 on v4

--- a/solution.py
+++ b/solution.py
@@ -470,7 +470,7 @@
             dma((n,)), dma((n,)), dma((n,)), dma((n,)), dma((8,)), dma((8,)),
         ],
         compiler_params=pltpu.CompilerParams(
-            collective_id=0, has_side_effects=True, vmem_limit_bytes=40 * 1024 * 1024
+            collective_id=0, has_side_effects=True, vmem_limit_bytes=56 * 1024 * 1024
         ),
         cost_estimate=pl.CostEstimate(
             flops=10**9, bytes_accessed=2 * 10**6, transcendentals=0

time: 39.3 us -> 37.5 us (0.954)
  local copies, waits for them, and re-layouts: 4.41 us -> 2.14 us
  Pallas kernels: 34.5 us -> 35.1 us
    unnamed x22 -> x16, local copies, waits for them, and re-layouts: 3.35 us -> 1.08 us
    pallas_call x1, Pallas kernels: 21.6 us -> 22.2 us  [regrid(): pl.pallas_call(functools.partial(regrid_kernel, tile_rows, tile_cols), ou...]
where the time goes in v5:
time: 37.5 us; the launch traced here: 37.4 us
  Pallas kernels  35.1 us (94%)
  local copies, waits for them, and re-layouts  2.14 us (6%)
    pallas_call x1, Pallas kernels, regrid(): pl.pallas_call(functools.partial(regrid_kernel, tile_rows, tile_cols), ou...  22.2 us
    pallas_call x1, Pallas kernels, unet(): pl.pallas_call(functools.partial(unet_kernel, tile_rows, tile_cols), out_...  13 us
    unnamed x16, local copies, waits for them, and re-layouts  1.08 us
    reshape x1, local copies, waits for them, and re-layouts, body(): return result.reshape(tile_rows, tile_cols, 2, FIELDS)  1.06 us

profile of v5, /device:TPU:0, one launch (start us, length us, event | category | flops | bytes accessed | tf_op | source)
XLA Modules:
  0.0 37.4 jit_solution(715196174473153236)
XLA Ops:
  0.0 0.0 copy-start
  0.0 0.0 copy-start.1
  0.0 0.0 copy-start.2
  0.0 0.0 copy-start.3
  0.0 0.0 copy-start.4
  0.0 0.0 copy-start.5
  0.0 0.0 copy-start.6
  0.0 22.2 %shard_map.109.p_ref = bf16[2304,128]{1,0:T(8,128)(2,1)} custom-call(bf16[1024,128]{1,0:T(8,128)(2,1)} %bitcast.6, s32[8,256]{1,0:T(8,128)} %bitcast.9, s32[32,4,32]{2,1,0:T(4,128)} %bitcast.7, f32[32,4,32]{2,1,0:T(4,128)} %bitcast.8), custom_call_target="tpu_custom_call" | custom-call | flops 1000000000 | bytes 2000000 | tf_op jit(solution)/shard_map/pallas_call | solution.py:450
  22.2 0.0 copy-done
  22.2 0.0 copy-done.1
  22.2 0.0 copy-done.2
  22.3 0.0 copy-done.3
  22.3 0.0 copy-done.4
  22.3 0.0 copy-done.5
  22.3 0.0 copy-done.6
  22.3 0.0 copy-start.7
  22.3 1.1 %copy-done.7 = bf16[2304,128]{1,0:T(8,128)(2,1)S(1)} copy-done((bf16[2304,128]{1,0:T(8,128)(2,1)S(1)}, bf16[2304,128]{1,0:T(8,128)(2,1)}, u32[]{:S(2)}) %copy-start.7) | copy-done | bytes 589848
  23.4 13.0 %shard_map.110 = bf16[1024,128]{1,0:T(8,128)(2,1)S(1)} custom-call(bf16[2304,128]{1,0:T(8,128)(2,1)S(1)} %copy-done.7, bf16[3,3,64,128]{3,2,1,0:T(8,128)(2,1)S(1)} %copy-done.5, bf16[3,3,128,128]{3,2,1,0:T(8,128)(2,1)S(1)} %copy-done.1, bf16[3,3,128,128]{3,2,1,0:T(8,128)(2,1)S(1)} %copy-done.2, bf16[3,3,128,128]{3,2,1,0:T(8,128)(2,1)S(1)} %copy-done.3, ...), custom_call_target="tpu_custom_call" | custom-call | flops 6000000000 | bytes 4000000 | tf_op jit(solution)/shard_map/pallas_call | solution.py:185
  36.3 1.1 %reshape.11 = bf16[32,32,2,64]{3,2,1,0:T(2,128)(2,1)} reshape(bf16[1024,128]{1,0:T(8,128)(2,1)S(1)} %shard_map.110) | data formatting | bytes 524288 | tf_op jit(solution)/shard_map/reshape | solution.py:493
Async XLA Ops:
  0.0 22.2 %copy-start = (bf16[3,3,256,128]{3,2,1,0:T(8,128)(2,1)S(1)}, bf16[3,3,256,128]{3,2,1,0:T(8,128)(2,1)}, u32[]{:S(2)}) copy-start(bf16[3,3,256,128]{3,2,1,0:T(8,128)(2,1)} %w_d1.1) | copy-start | bytes 1769476
  0.0 22.2 %copy-start.1 = (bf16[3,3,128,128]{3,2,1,0:T(8,128)(2,1)S(1)}, bf16[3,3,128,128]{3,2,1,0:T(8,128)(2,1)}, u32[]{:S(2)}) copy-start(bf16[3,3,128,128]{3,2,1,0:T(8,128)(2,1)} %w_enc.1) | copy-start | bytes 884740
  0.0 22.2 %copy-start.2 = (bf16[3,3,128,128]{3,2,1,0:T(8,128)(2,1)S(1)}, bf16[3,3,128,128]{3,2,1,0:T(8,128)(2,1)}, u32[]{:S(2)}) copy-start(bf16[3,3,128,128]{3,2,1,0:T(8,128)(2,1)} %w_m1.1) | copy-start | bytes 884740
  0.0 22.3 %copy-start.3 = (bf16[3,3,128,128]{3,2,1,0:T(8,128)(2,1)S(1)}, bf16[3,3,128,128]{3,2,1,0:T(8,128)(2,1)}, u32[]{:S(2)}) copy-start(bf16[3,3,128,128]{3,2,1,0:T(8,128)(2,1)} %w_m2.1) | copy-start | bytes 884740
  0.0 22.3 %copy-start.4 = (bf16[3,3,128,128]{3,2,1,0:T(8,128)(2,1)S(1)}, bf16[3,3,128,128]{3,2,1,0:T(8,128)(2,1)}, u32[]{:S(2)}) copy-start(bf16[3,3,128,128]{3,2,1,0:T(8,128)(2,1)} %w_d2.1) | copy-start | bytes 884740
  0.0 22.3 %copy-start.5 = (bf16[3,3,64,128]{3,2,1,0:T(8,128)(2,1)S(1)}, bf16[3,3,64,128]{3,2,1,0:T(8,128)(2,1)}, u32[]{:S(2)}) copy-start(bf16[3,3,64,128]{3,2,1,0:T(8,128)(2,1)} %w_in.1) | copy-start | bytes 442372
  0.0 22.3 %copy-start.6 = (bf16[128,64]{0,1:T(8,128)(2,1)S(1)}, bf16[128,64]{0,1:T(8,128)(2,1)}, u32[]{:S(2)}) copy-start(bf16[128,64]{0,1:T(8,128)(2,1)} %param.21) | copy-start | bytes 49156
  22.3 1.1 %copy-start.7 = (bf16[2304,128]{1,0:T(8,128)(2,1)S(1)}, bf16[2304,128]{1,0:T(8,128)(2,1)}, u32[]{:S(2)}) copy-start(bf16[2304,128]{1,0:T(8,128)(2,1)} %shard_map.109.p_ref) | copy-start | bytes 1769476
